TPU v7x, 512 devices: a whole 4x8x8 slice. The times are simulated.
512 devices in a mesh: lon: 32 (over z, y_lo), lat: 16 (over x, y_hi, core).
Axes of the slice: x: 4, y: 8 (y_hi: 2, y_lo: 4; y = y_hi * 4 + y_lo), z: 8, core: 2. Of those that a mesh axis runs over, the one named last changes fastest.
Arguments:
- cotangent: float32 [4, 2048, 4096], P(None, 'lat', 'lon'), may hold values from -6 to 6
- coefficients: bfloat16 [9, 4, 2048, 4096], P(None, None, 'lat', 'lon'), may hold values from -2 to 2
- wet_mask: int32 [4, 2048, 4096], P(None, 'lat', 'lon'), may hold values 0 or 1
Outputs:
- gradient: float32 [4, 2048, 4096], P(None, 'lat', 'lon')
All inputs are finite; a program needn't handle non-finite values. No bound on the sum of `wet_mask` on one device may be relied on, other than what follows from the above.
Results may differ from a plain program's by a relative error of at most 0.0003.
Values sent between devices are 32-bit elements; how exact they have to be, the bound alone decides.
No kernel may reach another device: no remote copies, remote signals or barrier semaphores. Data moves between devices by JAX's collectives and lax.ppermute only.
A program may use at most 64 MiB of HBM per device.

v0:
```python
import jax
import jax.numpy as jnp
from jax import lax
from jax.sharding import PartitionSpec as P

ITERS = 8


NEIGHBOURS = [(-1, -1), (-1, 0), (-1, 1), (0, -1), (0, 1), (1, -1), (1, 0), (1, 1)]


def swapped(array, axis, distance):
    return lax.ppermute(array, axis, [(i, i ^ 1 << distance) for i in range(lax.axis_size(axis))])


def extended_2(array, sides, width):
    for axis, dim in sides:
        size, length = (lax.axis_size(axis), array.shape[dim])
        up = [(i, (i + 1) % size) for i in range(size)]
        down = [(j, i) for i, j in up]
        last = lax.slice_in_dim(array, length - width, length, axis=dim)
        leading = lax.slice_in_dim(array, 0, width, axis=dim)
        before = lax.ppermute(last, axis, up)
        after = lax.ppermute(leading, axis, down)
        array = jnp.concatenate([before, array, after], axis=dim)
    return array


def mirror(top_piece):
    places = lax.axis_size("lon")
    mirrored = top_piece
    for bit_number in range(places.bit_length() - 1):
        mirrored = swapped(mirrored, "lon", bit_number)
    return mirrored


def finish_rows(padded, row_count, depth):
    top_piece = padded[:, :, row_count + depth - 1 : row_count + depth, ::-1]
    mirrored = mirror(top_piece)
    lat_index = lax.axis_index("lat")
    top_index = lax.axis_size("lat") - 1
    above = padded[:, :, row_count + depth :, :]
    fold_rows = jnp.concatenate([mirrored, jnp.zeros_like(above[:, :, 1:, :])], axis=2)
    upper_rim = jnp.where(lat_index == top_index, fold_rows, above)
    below = padded[:, :, :depth, :]
    lower_rim = jnp.where(lat_index == 0, jnp.zeros_like(below), below)
    return jnp.concatenate(
        [lower_rim, padded[:, :, depth : row_count + depth, :], upper_rim], axis=2
    )


def extend(fields):
    row_count = fields.shape[2]
    padded = extended_2(fields, (("lon", 3), ("lat", 2)), 1)
    return finish_rows(padded, row_count, 1)


def combine(extended, centre, num_rows, num_cols):
    total = centre
    for number, (row_step, col_step) in enumerate(NEIGHBOURS):
        total = (
            total
            + extended[
                number,
                :,
                1 - row_step : 1 - row_step + num_rows,
                1 - col_step : 1 - col_step + num_cols,
            ]
        )
    return total


def shards(cotangent, coefficients, wet_mask):
    wet = wet_mask.astype(jnp.float32)
    num_rows, num_cols = (cotangent.shape[1], cotangent.shape[2])
    field = cotangent
    for iteration in range(ITERS):
        products = coefficients.astype(jnp.float32) * (wet * field)[None]
        beside_all = jnp.concatenate([products[:4], products[5:]], axis=0)
        extended = extend(beside_all)
        field = wet * combine(extended, products[4], num_rows, num_cols)
    return field


def solution(mesh):
    in_specs = (P(None, "lat", "lon"), P(None, None, "lat", "lon"), P(None, "lat", "lon"))
    out_specs = P(None, "lat", "lon")
    return jax.shard_map(shards, mesh=mesh, in_specs=in_specs, out_specs=out_specs, check_vma=False)
```

profile of v0, /device:TPU:80, one launch (start us, length us, event | category | flops | bytes accessed | tf_op | source)
XLA Modules:
  0.0 576.4 jit_solution(2318560088731308140)
XLA Ops:
  21.9 6.6 %collective-permute-start.2 = (f32[8,4,1,130]{3,0,2,1:T(8,128)S(1)}, f32[8,4,1,130]{3,0,2,1:T(8,128)S(1)}, u32[]{:S(2)}, u32[]{:S(2)}) collective-permute-start(f32[8,4,1,130]{3,0,2,1:T(8,128)S(1)} %copy.186), channel_id=1, source_target_pairs={{0,16},{16,0},{32,48},{48,32},{64,80},{80,64},{96,112},{112,96},{1... | collective-permute-start | bytes 49928 | tf_op jit(solution)/shard_map/ppermute | solution.py:13
  32.3 4.8 collective-permute-done.3
  43.4 7.9 %collective-permute-start.5 = (f32[8,4,1,130]{3,0,2,1:T(8,128)S(1)}, f32[8,4,1,130]{3,0,2,1:T(8,128)S(1)}, u32[]{:S(2)}, u32[]{:S(2)}) collective-permute-start(f32[8,4,1,130]{3,0,2,1:T(8,128)S(1)} %collective-permute-done.4), channel_id=1, source_target_pairs={{0,128},{16,144},{32,160},{48,176},{64,192},{80,208},{96,224},{112... | collective-permute-start | bytes 49928 | tf_op jit(solution)/shard_map/ppermute | solution.py:13
  53.3 9.7 %collective-permute-start.7 = (f32[8,4,1,130]{3,0,2,1:T(8,128)S(1)}, f32[8,4,1,130]{3,0,2,1:T(8,128)S(1)}, u32[]{:S(2)}, u32[]{:S(2)}) collective-permute-start(f32[8,4,1,130]{3,0,2,1:T(8,128)S(1)} %copy.187), channel_id=1, source_target_pairs={{1,0},{2,1},{3,2},{4,3},{5,4},{6,5},{7,6},{8,7},{9,8},{10,9},{11,1... | collective-permute-start | bytes 49928 | tf_op jit(solution)/shard_map/ppermute | solution.py:24
  63.0 5.0 collective-permute-start.6
  68.1 4.6 collective-permute-done.6
  95.9 4.6 collective-permute-start.11
  104.5 4.8 collective-permute-done.12
  121.5 9.7 %collective-permute-start.16 = (f32[8,4,1,130]{3,0,2,1:T(8,128)S(1)}, f32[8,4,1,130]{3,0,2,1:T(8,128)S(1)}, u32[]{:S(2)}, u32[]{:S(2)}) collective-permute-start(f32[8,4,1,130]{3,0,2,1:T(8,128)S(1)} %copy.199), channel_id=1, source_target_pairs={{1,0},{2,1},{3,2},{4,3},{5,4},{6,5},{7,6},{8,7},{9,8},{10,9},{11,1... | collective-permute-start | bytes 49928 | tf_op jit(solution)/shard_map/ppermute | solution.py:24
  135.6 5.5 collective-permute-done.15
  168.4 4.6 collective-permute-start.20
  193.3 9.7 %collective-permute-start.25 = (f32[8,4,1,130]{3,0,2,1:T(8,128)S(1)}, f32[8,4,1,130]{3,0,2,1:T(8,128)S(1)}, u32[]{:S(2)}, u32[]{:S(2)}) collective-permute-start(f32[8,4,1,130]{3,0,2,1:T(8,128)S(1)} %copy.211), channel_id=1, source_target_pairs={{1,0},{2,1},{3,2},{4,3},{5,4},{6,5},{7,6},{8,7},{9,8},{10,9},{11,1... | collective-permute-start | bytes 49928 | tf_op jit(solution)/shard_map/ppermute | solution.py:24
  203.0 5.0 collective-permute-start.24
  208.1 4.7 collective-permute-done.24
  239.6 4.9 collective-permute-start.29
  248.3 4.7 collective-permute-done.30
  258.9 4.6 collective-permute-start.32
  265.5 9.7 %collective-permute-start.34 = (f32[8,4,1,130]{3,0,2,1:T(8,128)S(1)}, f32[8,4,1,130]{3,0,2,1:T(8,128)S(1)}, u32[]{:S(2)}, u32[]{:S(2)}) collective-permute-start(f32[8,4,1,130]{3,0,2,1:T(8,128)S(1)} %copy.223), channel_id=1, source_target_pairs={{1,0},{2,1},{3,2},{4,3},{5,4},{6,5},{7,6},{8,7},{9,8},{10,9},{11,1... | collective-permute-start | bytes 49928 | tf_op jit(solution)/shard_map/ppermute | solution.py:24
  275.1 5.3 collective-permute-start.33
  311.9 4.7 collective-permute-start.38
  337.6 9.7 %collective-permute-start.43 = (f32[8,4,1,130]{3,0,2,1:T(8,128)S(1)}, f32[8,4,1,130]{3,0,2,1:T(8,128)S(1)}, u32[]{:S(2)}, u32[]{:S(2)}) collective-permute-start(f32[8,4,1,130]{3,0,2,1:T(8,128)S(1)} %copy.235), channel_id=1, source_target_pairs={{1,0},{2,1},{3,2},{4,3},{5,4},{6,5},{7,6},{8,7},{9,8},{10,9},{11,1... | collective-permute-start | bytes 49928 | tf_op jit(solution)/shard_map/ppermute | solution.py:24
  351.7 5.3 collective-permute-done.42
  409.3 9.7 %collective-permute-start.52 = (f32[8,4,1,130]{3,0,2,1:T(8,128)S(1)}, f32[8,4,1,130]{3,0,2,1:T(8,128)S(1)}, u32[]{:S(2)}, u32[]{:S(2)}) collective-permute-start(f32[8,4,1,130]{3,0,2,1:T(8,128)S(1)} %copy.247), channel_id=1, source_target_pairs={{1,0},{2,1},{3,2},{4,3},{5,4},{6,5},{7,6},{8,7},{9,8},{10,9},{11,1... | collective-permute-start | bytes 49928 | tf_op jit(solution)/shard_map/ppermute | solution.py:24
  419.0 4.9 collective-permute-start.51
  424.0 4.8 collective-permute-done.51
  480.8 9.7 %collective-permute-start.61 = (f32[8,4,1,130]{3,0,2,1:T(8,128)S(1)}, f32[8,4,1,130]{3,0,2,1:T(8,128)S(1)}, u32[]{:S(2)}, u32[]{:S(2)}) collective-permute-start(f32[8,4,1,130]{3,0,2,1:T(8,128)S(1)} %copy.259), channel_id=1, source_target_pairs={{1,0},{2,1},{3,2},{4,3},{5,4},{6,5},{7,6},{8,7},{9,8},{10,9},{11,1... | collective-permute-start | bytes 49928 | tf_op jit(solution)/shard_map/ppermute | solution.py:24
  490.5 5.3 collective-permute-start.60
  495.9 4.7 collective-permute-done.60
  536.1 4.6 collective-permute-done.66
  552.9 9.7 %collective-permute-start.70 = (f32[8,4,1,130]{3,0,2,1:T(8,128)S(1)}, f32[8,4,1,130]{3,0,2,1:T(8,128)S(1)}, u32[]{:S(2)}, u32[]{:S(2)}) collective-permute-start(f32[8,4,1,130]{3,0,2,1:T(8,128)S(1)} %copy.271), channel_id=1, source_target_pairs={{1,0},{2,1},{3,2},{4,3},{5,4},{6,5},{7,6},{8,7},{9,8},{10,9},{11,1... | collective-permute-start | bytes 49928 | tf_op jit(solution)/shard_map/ppermute | solution.py:24
  562.6 4.8 collective-permute-start.69
  567.5 5.0 collective-permute-done.69
  (267 shorter events, 375.5 us)
Async XLA Ops:
  43.4 19.6 %collective-permute-start.5 = (f32[8,4,1,130]{3,0,2,1:T(8,128)S(1)}, f32[8,4,1,130]{3,0,2,1:T(8,128)S(1)}, u32[]{:S(2)}, u32[]{:S(2)}) collective-permute-start(f32[8,4,1,130]{3,0,2,1:T(8,128)S(1)} %collective-permute-done.4), channel_id=1, source_target_pairs={{0,128},{16,144},{32,160},{48,176},{64,192},{80,208},{96,224},{112... | collective-permute-start | bytes 49928 | tf_op jit(solution)/shard_map/ppermute | solution.py:13
  51.4 16.6 %collective-permute-start.8 = (f32[8,4,1,130]{3,0,2,1:T(8,128)S(1)}, f32[8,4,1,130]{3,0,2,1:T(8,128)S(1)}, u32[]{:S(2)}, u32[]{:S(2)}) collective-permute-start(f32[8,4,1,130]{3,0,2,1:T(8,128)S(1)} %copy.192), channel_id=1, source_target_pairs={{0,1},{1,2},{2,3},{3,4},{4,5},{5,6},{6,7},{7,8},{8,9},{9,10},{10,1... | collective-permute-start | bytes 49928 | tf_op jit(solution)/shard_map/ppermute | solution.py:23
  53.3 14.7 %collective-permute-start.7 = (f32[8,4,1,130]{3,0,2,1:T(8,128)S(1)}, f32[8,4,1,130]{3,0,2,1:T(8,128)S(1)}, u32[]{:S(2)}, u32[]{:S(2)}) collective-permute-start(f32[8,4,1,130]{3,0,2,1:T(8,128)S(1)} %copy.187), channel_id=1, source_target_pairs={{1,0},{2,1},{3,2},{4,3},{5,4},{6,5},{7,6},{8,7},{9,8},{10,9},{11,1... | collective-permute-start | bytes 49928 | tf_op jit(solution)/shard_map/ppermute | solution.py:24
  63.0 9.7 %collective-permute-start.6 = (f32[8,4,1,130]{3,0,2,1:T(8,128)S(1)}, f32[8,4,1,130]{3,0,2,1:T(8,128)S(1)}, u32[]{:S(2)}, u32[]{:S(2)}) collective-permute-start(f32[8,4,1,130]{3,0,2,1:T(8,128)S(1)} %collective-permute-done.5), channel_id=1, source_target_pairs={{0,256},{16,272},{32,288},{48,304},{64,320},{80,336},{96,352},{112... | collective-permute-start | bytes 49928 | tf_op jit(solution)/shard_map/ppermute | solution.py:13
  115.1 16.1 %collective-permute-start.14 = (f32[8,4,1,130]{3,0,2,1:T(8,128)S(1)}, f32[8,4,1,130]{3,0,2,1:T(8,128)S(1)}, u32[]{:S(2)}, u32[]{:S(2)}) collective-permute-start(f32[8,4,1,130]{3,0,2,1:T(8,128)S(1)} %collective-permute-done.13), channel_id=1, source_target_pairs={{0,128},{16,144},{32,160},{48,176},{64,192},{80,208},{96,224},{112... | collective-permute-start | bytes 49928 | tf_op jit(solution)/shard_map/ppermute | solution.py:13
  119.5 15.9 %collective-permute-start.17 = (f32[8,4,1,130]{3,0,2,1:T(8,128)S(1)}, f32[8,4,1,130]{3,0,2,1:T(8,128)S(1)}, u32[]{:S(2)}, u32[]{:S(2)}) collective-permute-start(f32[8,4,1,130]{3,0,2,1:T(8,128)S(1)} %copy.204), channel_id=1, source_target_pairs={{0,1},{1,2},{2,3},{3,4},{4,5},{5,6},{6,7},{7,8},{8,9},{9,10},{10,1... | collective-permute-start | bytes 49928 | tf_op jit(solution)/shard_map/ppermute | solution.py:23
  121.5 14.1 %collective-permute-start.16 = (f32[8,4,1,130]{3,0,2,1:T(8,128)S(1)}, f32[8,4,1,130]{3,0,2,1:T(8,128)S(1)}, u32[]{:S(2)}, u32[]{:S(2)}) collective-permute-start(f32[8,4,1,130]{3,0,2,1:T(8,128)S(1)} %copy.199), channel_id=1, source_target_pairs={{1,0},{2,1},{3,2},{4,3},{5,4},{6,5},{7,6},{8,7},{9,8},{10,9},{11,1... | collective-permute-start | bytes 49928 | tf_op jit(solution)/shard_map/ppermute | solution.py:24
  131.2 9.9 %collective-permute-start.15 = (f32[8,4,1,130]{3,0,2,1:T(8,128)S(1)}, f32[8,4,1,130]{3,0,2,1:T(8,128)S(1)}, u32[]{:S(2)}, u32[]{:S(2)}) collective-permute-start(f32[8,4,1,130]{3,0,2,1:T(8,128)S(1)} %collective-permute-done.14), channel_id=1, source_target_pairs={{0,256},{16,272},{32,288},{48,304},{64,320},{80,336},{96,352},{112... | collective-permute-start | bytes 49928 | tf_op jit(solution)/shard_map/ppermute | solution.py:13
  187.4 15.6 %collective-permute-start.23 = (f32[8,4,1,130]{3,0,2,1:T(8,128)S(1)}, f32[8,4,1,130]{3,0,2,1:T(8,128)S(1)}, u32[]{:S(2)}, u32[]{:S(2)}) collective-permute-start(f32[8,4,1,130]{3,0,2,1:T(8,128)S(1)} %collective-permute-done.22), channel_id=1, source_target_pairs={{0,128},{16,144},{32,160},{48,176},{64,192},{80,208},{96,224},{112... | collective-permute-start | bytes 49928 | tf_op jit(solution)/shard_map/ppermute | solution.py:13
  191.4 16.6 %collective-permute-start.26 = (f32[8,4,1,130]{3,0,2,1:T(8,128)S(1)}, f32[8,4,1,130]{3,0,2,1:T(8,128)S(1)}, u32[]{:S(2)}, u32[]{:S(2)}) collective-permute-start(f32[8,4,1,130]{3,0,2,1:T(8,128)S(1)} %copy.216), channel_id=1, source_target_pairs={{0,1},{1,2},{2,3},{3,4},{4,5},{5,6},{6,7},{7,8},{8,9},{9,10},{10,1... | collective-permute-start | bytes 49928 | tf_op jit(solution)/shard_map/ppermute | solution.py:23
  193.3 14.7 %collective-permute-start.25 = (f32[8,4,1,130]{3,0,2,1:T(8,128)S(1)}, f32[8,4,1,130]{3,0,2,1:T(8,128)S(1)}, u32[]{:S(2)}, u32[]{:S(2)}) collective-permute-start(f32[8,4,1,130]{3,0,2,1:T(8,128)S(1)} %copy.211), channel_id=1, source_target_pairs={{1,0},{2,1},{3,2},{4,3},{5,4},{6,5},{7,6},{8,7},{9,8},{10,9},{11,1... | collective-permute-start | bytes 49928 | tf_op jit(solution)/shard_map/ppermute | solution.py:24
  203.0 9.7 %collective-permute-start.24 = (f32[8,4,1,130]{3,0,2,1:T(8,128)S(1)}, f32[8,4,1,130]{3,0,2,1:T(8,128)S(1)}, u32[]{:S(2)}, u32[]{:S(2)}) collective-permute-start(f32[8,4,1,130]{3,0,2,1:T(8,128)S(1)} %collective-permute-done.23), channel_id=1, source_target_pairs={{0,256},{16,272},{32,288},{48,304},{64,320},{80,336},{96,352},{112... | collective-permute-start | bytes 49928 | tf_op jit(solution)/shard_map/ppermute | solution.py:13
  258.9 16.3 %collective-permute-start.32 = (f32[8,4,1,130]{3,0,2,1:T(8,128)S(1)}, f32[8,4,1,130]{3,0,2,1:T(8,128)S(1)}, u32[]{:S(2)}, u32[]{:S(2)}) collective-permute-start(f32[8,4,1,130]{3,0,2,1:T(8,128)S(1)} %collective-permute-done.31), channel_id=1, source_target_pairs={{0,128},{16,144},{32,160},{48,176},{64,192},{80,208},{96,224},{112... | collective-permute-start | bytes 49928 | tf_op jit(solution)/shard_map/ppermute | solution.py:13
  263.5 17.0 %collective-permute-start.35 = (f32[8,4,1,130]{3,0,2,1:T(8,128)S(1)}, f32[8,4,1,130]{3,0,2,1:T(8,128)S(1)}, u32[]{:S(2)}, u32[]{:S(2)}) collective-permute-start(f32[8,4,1,130]{3,0,2,1:T(8,128)S(1)} %copy.228), channel_id=1, source_target_pairs={{0,1},{1,2},{2,3},{3,4},{4,5},{5,6},{6,7},{7,8},{8,9},{9,10},{10,1... | collective-permute-start | bytes 49928 | tf_op jit(solution)/shard_map/ppermute | solution.py:23
  265.5 15.1 %collective-permute-start.34 = (f32[8,4,1,130]{3,0,2,1:T(8,128)S(1)}, f32[8,4,1,130]{3,0,2,1:T(8,128)S(1)}, u32[]{:S(2)}, u32[]{:S(2)}) collective-permute-start(f32[8,4,1,130]{3,0,2,1:T(8,128)S(1)} %copy.223), channel_id=1, source_target_pairs={{1,0},{2,1},{3,2},{4,3},{5,4},{6,5},{7,6},{8,7},{9,8},{10,9},{11,1... | collective-permute-start | bytes 49928 | tf_op jit(solution)/shard_map/ppermute | solution.py:24
  275.1 9.7 %collective-permute-start.33 = (f32[8,4,1,130]{3,0,2,1:T(8,128)S(1)}, f32[8,4,1,130]{3,0,2,1:T(8,128)S(1)}, u32[]{:S(2)}, u32[]{:S(2)}) collective-permute-start(f32[8,4,1,130]{3,0,2,1:T(8,128)S(1)} %collective-permute-done.32), channel_id=1, source_target_pairs={{0,256},{16,272},{32,288},{48,304},{64,320},{80,336},{96,352},{112... | collective-permute-start | bytes 49928 | tf_op jit(solution)/shard_map/ppermute | solution.py:13
  331.0 16.2 %collective-permute-start.41 = (f32[8,4,1,130]{3,0,2,1:T(8,128)S(1)}, f32[8,4,1,130]{3,0,2,1:T(8,128)S(1)}, u32[]{:S(2)}, u32[]{:S(2)}) collective-permute-start(f32[8,4,1,130]{3,0,2,1:T(8,128)S(1)} %collective-permute-done.40), channel_id=1, source_target_pairs={{0,128},{16,144},{32,160},{48,176},{64,192},{80,208},{96,224},{112... | collective-permute-start | bytes 49928 | tf_op jit(solution)/shard_map/ppermute | solution.py:13
  335.6 16.0 %collective-permute-start.44 = (f32[8,4,1,130]{3,0,2,1:T(8,128)S(1)}, f32[8,4,1,130]{3,0,2,1:T(8,128)S(1)}, u32[]{:S(2)}, u32[]{:S(2)}) collective-permute-start(f32[8,4,1,130]{3,0,2,1:T(8,128)S(1)} %copy.240), channel_id=1, source_target_pairs={{0,1},{1,2},{2,3},{3,4},{4,5},{5,6},{6,7},{7,8},{8,9},{9,10},{10,1... | collective-permute-start | bytes 49928 | tf_op jit(solution)/shard_map/ppermute | solution.py:23
  337.6 14.1 %collective-permute-start.43 = (f32[8,4,1,130]{3,0,2,1:T(8,128)S(1)}, f32[8,4,1,130]{3,0,2,1:T(8,128)S(1)}, u32[]{:S(2)}, u32[]{:S(2)}) collective-permute-start(f32[8,4,1,130]{3,0,2,1:T(8,128)S(1)} %copy.235), channel_id=1, source_target_pairs={{1,0},{2,1},{3,2},{4,3},{5,4},{6,5},{7,6},{8,7},{9,8},{10,9},{11,1... | collective-permute-start | bytes 49928 | tf_op jit(solution)/shard_map/ppermute | solution.py:24
  347.3 9.7 %collective-permute-start.42 = (f32[8,4,1,130]{3,0,2,1:T(8,128)S(1)}, f32[8,4,1,130]{3,0,2,1:T(8,128)S(1)}, u32[]{:S(2)}, u32[]{:S(2)}) collective-permute-start(f32[8,4,1,130]{3,0,2,1:T(8,128)S(1)} %collective-permute-done.41), channel_id=1, source_target_pairs={{0,256},{16,272},{32,288},{48,304},{64,320},{80,336},{96,352},{112... | collective-permute-start | bytes 49928 | tf_op jit(solution)/shard_map/ppermute | solution.py:13
  402.9 16.2 %collective-permute-start.50 = (f32[8,4,1,130]{3,0,2,1:T(8,128)S(1)}, f32[8,4,1,130]{3,0,2,1:T(8,128)S(1)}, u32[]{:S(2)}, u32[]{:S(2)}) collective-permute-start(f32[8,4,1,130]{3,0,2,1:T(8,128)S(1)} %collective-permute-done.49), channel_id=1, source_target_pairs={{0,128},{16,144},{32,160},{48,176},{64,192},{80,208},{96,224},{112... | collective-permute-start | bytes 49928 | tf_op jit(solution)/shard_map/ppermute | solution.py:13
  407.4 16.6 %collective-permute-start.53 = (f32[8,4,1,130]{3,0,2,1:T(8,128)S(1)}, f32[8,4,1,130]{3,0,2,1:T(8,128)S(1)}, u32[]{:S(2)}, u32[]{:S(2)}) collective-permute-start(f32[8,4,1,130]{3,0,2,1:T(8,128)S(1)} %copy.252), channel_id=1, source_target_pairs={{0,1},{1,2},{2,3},{3,4},{4,5},{5,6},{6,7},{7,8},{8,9},{9,10},{10,1... | collective-permute-start | bytes 49928 | tf_op jit(solution)/shard_map/ppermute | solution.py:23
  409.3 14.7 %collective-permute-start.52 = (f32[8,4,1,130]{3,0,2,1:T(8,128)S(1)}, f32[8,4,1,130]{3,0,2,1:T(8,128)S(1)}, u32[]{:S(2)}, u32[]{:S(2)}) collective-permute-start(f32[8,4,1,130]{3,0,2,1:T(8,128)S(1)} %copy.247), channel_id=1, source_target_pairs={{1,0},{2,1},{3,2},{4,3},{5,4},{6,5},{7,6},{8,7},{9,8},{10,9},{11,1... | collective-permute-start | bytes 49928 | tf_op jit(solution)/shard_map/ppermute | solution.py:24
  419.0 9.8 %collective-permute-start.51 = (f32[8,4,1,130]{3,0,2,1:T(8,128)S(1)}, f32[8,4,1,130]{3,0,2,1:T(8,128)S(1)}, u32[]{:S(2)}, u32[]{:S(2)}) collective-permute-start(f32[8,4,1,130]{3,0,2,1:T(8,128)S(1)} %collective-permute-done.50), channel_id=1, source_target_pairs={{0,256},{16,272},{32,288},{48,304},{64,320},{80,336},{96,352},{112... | collective-permute-start | bytes 49928 | tf_op jit(solution)/shard_map/ppermute | solution.py:13
  474.7 15.8 %collective-permute-start.59 = (f32[8,4,1,130]{3,0,2,1:T(8,128)S(1)}, f32[8,4,1,130]{3,0,2,1:T(8,128)S(1)}, u32[]{:S(2)}, u32[]{:S(2)}) collective-permute-start(f32[8,4,1,130]{3,0,2,1:T(8,128)S(1)} %collective-permute-done.58), channel_id=1, source_target_pairs={{0,128},{16,144},{32,160},{48,176},{64,192},{80,208},{96,224},{112... | collective-permute-start | bytes 49928 | tf_op jit(solution)/shard_map/ppermute | solution.py:13
  478.9 16.9 %collective-permute-start.62 = (f32[8,4,1,130]{3,0,2,1:T(8,128)S(1)}, f32[8,4,1,130]{3,0,2,1:T(8,128)S(1)}, u32[]{:S(2)}, u32[]{:S(2)}) collective-permute-start(f32[8,4,1,130]{3,0,2,1:T(8,128)S(1)} %copy.264), channel_id=1, source_target_pairs={{0,1},{1,2},{2,3},{3,4},{4,5},{5,6},{6,7},{7,8},{8,9},{9,10},{10,1... | collective-permute-start | bytes 49928 | tf_op jit(solution)/shard_map/ppermute | solution.py:23
  480.8 15.1 %collective-permute-start.61 = (f32[8,4,1,130]{3,0,2,1:T(8,128)S(1)}, f32[8,4,1,130]{3,0,2,1:T(8,128)S(1)}, u32[]{:S(2)}, u32[]{:S(2)}) collective-permute-start(f32[8,4,1,130]{3,0,2,1:T(8,128)S(1)} %copy.259), channel_id=1, source_target_pairs={{1,0},{2,1},{3,2},{4,3},{5,4},{6,5},{7,6},{8,7},{9,8},{10,9},{11,1... | collective-permute-start | bytes 49928 | tf_op jit(solution)/shard_map/ppermute | solution.py:24
  490.5 10.1 %collective-permute-start.60 = (f32[8,4,1,130]{3,0,2,1:T(8,128)S(1)}, f32[8,4,1,130]{3,0,2,1:T(8,128)S(1)}, u32[]{:S(2)}, u32[]{:S(2)}) collective-permute-start(f32[8,4,1,130]{3,0,2,1:T(8,128)S(1)} %collective-permute-done.59), channel_id=1, source_target_pairs={{0,256},{16,272},{32,288},{48,304},{64,320},{80,336},{96,352},{112... | collective-permute-start | bytes 49928 | tf_op jit(solution)/shard_map/ppermute | solution.py:13
  546.5 16.1 %collective-permute-start.68 = (f32[8,4,1,130]{3,0,2,1:T(8,128)S(1)}, f32[8,4,1,130]{3,0,2,1:T(8,128)S(1)}, u32[]{:S(2)}, u32[]{:S(2)}) collective-permute-start(f32[8,4,1,130]{3,0,2,1:T(8,128)S(1)} %collective-permute-done.67), channel_id=1, source_target_pairs={{0,128},{16,144},{32,160},{48,176},{64,192},{80,208},{96,224},{112... | collective-permute-start | bytes 49928 | tf_op jit(solution)/shard_map/ppermute | solution.py:13
  551.0 16.5 %collective-permute-start.71 = (f32[8,4,1,130]{3,0,2,1:T(8,128)S(1)}, f32[8,4,1,130]{3,0,2,1:T(8,128)S(1)}, u32[]{:S(2)}, u32[]{:S(2)}) collective-permute-start(f32[8,4,1,130]{3,0,2,1:T(8,128)S(1)} %copy.276), channel_id=1, source_target_pairs={{0,1},{1,2},{2,3},{3,4},{4,5},{5,6},{6,7},{7,8},{8,9},{9,10},{10,1... | collective-permute-start | bytes 49928 | tf_op jit(solution)/shard_map/ppermute | solution.py:23
  552.9 14.6 %collective-permute-start.70 = (f32[8,4,1,130]{3,0,2,1:T(8,128)S(1)}, f32[8,4,1,130]{3,0,2,1:T(8,128)S(1)}, u32[]{:S(2)}, u32[]{:S(2)}) collective-permute-start(f32[8,4,1,130]{3,0,2,1:T(8,128)S(1)} %copy.271), channel_id=1, source_target_pairs={{1,0},{2,1},{3,2},{4,3},{5,4},{6,5},{7,6},{8,7},{9,8},{10,9},{11,1... | collective-permute-start | bytes 49928 | tf_op jit(solution)/shard_map/ppermute | solution.py:24
  562.6 9.9 %collective-permute-start.69 = (f32[8,4,1,130]{3,0,2,1:T(8,128)S(1)}, f32[8,4,1,130]{3,0,2,1:T(8,128)S(1)}, u32[]{:S(2)}, u32[]{:S(2)}) collective-permute-start(f32[8,4,1,130]{3,0,2,1:T(8,128)S(1)} %collective-permute-done.68), channel_id=1, source_target_pairs={{0,256},{16,272},{32,288},{48,304},{64,320},{80,336},{96,352},{112... | collective-permute-start | bytes 49928 | tf_op jit(solution)/shard_map/ppermute | solution.py:13
  (49 other events, 349.7 us)
where the time goes:
time: 588 us; the launch traced here: 576 us
  starting transfers between devices  298 us (51%)
  waiting for transfers between devices  129 us (22%)
  local copies, waits for them, and re-layouts  78.1 us (13%)
  other arithmetic  69.7 us (12%)
    ppermute x40, starting transfers between devices, swapped(): lax.ppermute(array, axis, [(i, i ^ 1 << distance) for i in range(lax.axis...  158 us
    ppermute x40, waiting for transfers between devices, swapped(): lax.ppermute(array, axis, [(i, i ^ 1 << distance) for i in range(lax.axis...  113 us
    ppermute x16, starting transfers between devices, extended_2(): after = lax.ppermute(leading, axis, down)  93.9 us
    ppermute x16, starting transfers between devices, extended_2(): before = lax.ppermute(last, axis, up)  46.2 us
    mul x16, other arithmetic, shards(): products = coefficients.astype(jnp.float32) * (wet * field)[None]  34.4 us
    concatenate x8, other arithmetic, shards(): beside_all = jnp.concatenate([products[:4], products[5:]], axis=0)  20.3 us
    slice x16, local copies, waits for them, and re-layouts, extended_2(): last = lax.slice_in_dim(array, length - width, length, axis=dim)  17.7 us
    ppermute x8, local copies, waits for them, and re-layouts, extended_2(): after = lax.ppermute(leading, axis, down)  15.9 us
  transfers between devices with their start and end apart: 72, of which 40 were waited for; matrix products, arithmetic and copies ran while one was open for 5% of the time, Pallas kernels for 0%

commit v1 on v0

v1 whole, which is shorter than its diff:
```python
import jax
import jax.numpy as jnp
from jax import lax
from jax.experimental import pallas as pl
from jax.experimental.pallas import tpu as pltpu
from jax.sharding import PartitionSpec as P


STEPS = 8
LEVELS = 4
SIZE = 128
TILES = LEVELS + 1
F32 = jnp.float32


def dc_of(c):
    return c % 3 - 1


def lanes(rows):
    return lax.broadcasted_iota(jnp.int32, (rows, SIZE), 1)


def sublanes(rows):
    return lax.broadcasted_iota(jnp.int32, (rows, SIZE), 0)


def turn(x, shift, axis=1):
    shift = shift % x.shape[axis]
    return x if shift == 0 else pltpu.roll(x, shift, axis)


def seam(level, dc):
    return 16 * level + (8 if dc == 1 else 7)


def join(mains, rim, dc, lane):
    if dc == 0:
        return list(mains) + [rim]
    fixed, new_rim = [], rim
    for level in range(LEVELS):
        here = lane == seam(level, dc)
        fixed.append(jnp.where(here, rim, mains[level]))
        new_rim = jnp.where(here, mains[level], new_rim)
    return fixed + [new_rim]


def shifted(tiles, dc, lane):
    return join([turn(t, dc) for t in tiles[:LEVELS]], turn(tiles[LEVELS], dc), dc, lane)


def source(v, level, block, cot, coef, wet, is_top):
    rows = slice(16 * block, 16 * block + 16)
    if v == 9:
        return cot[level, rows, :]
    x = coef[v, level, rows, :].astype(F32)
    if block == SIZE // 16 - 1 and v >= 6:
        other = coef[8 - v, level, rows, :].astype(F32)
        x = jnp.where((sublanes(16) == 15) & is_top, other, x)
    return x * wet[level, rows, :].astype(F32)


def pack_lon(cot, coef, wet, pay1, pay2):
    is_top = lax.axis_index("lat") == lax.axis_size("lat") - 1
    even = lax.axis_index("lon") % 2 == 0
    lane = lanes(16)
    first = (lane & 8) == 0

    def both_edges(pair, block):
        out = None
        for half in (0, 1):
            for level in range(LEVELS):
                x = source(2 * pair + half, level, block, cot, coef, wet, is_top)
                x = turn(x, 64 * half + 16 * level + 8)
                out = x if out is None else jnp.where((lane >> 4) == 4 * half + level, x, out)
        return out

    def put(row, a, b):
        east = jnp.where(first, a, turn(b, 8))
        west = jnp.where(first, turn(b, -8), a)
        pay1[row : row + 16, :] = jnp.where(even, east, west)
        pay2[row : row + 16, :] = jnp.where(even, west, east)

    for block in range(8):
        put(16 * block, both_edges(0, block), both_edges(1, block))
        put(128 + 16 * block, both_edges(2, block), both_edges(3, block))
    for block in range(4):
        put(256 + 16 * block, both_edges(4, block), both_edges(4, block + 4))


def rotate_main(cot, coef, wet, token, out):
    del token
    is_top = lax.axis_index("lat") == lax.axis_size("lat") - 1
    for block in range(8):
        rows = slice(16 * block, 16 * block + 16)
        for v in range(10):
            for level in range(LEVELS):
                x = source(v, level, block, cot, coef, wet, is_top)
                if v < 9:
                    out[v, level, rows, :] = turn(x, 16 * level + 8 + dc_of(v))
                else:
                    for dc in (-1, 0, 1):
                        out[10 + dc, level, rows, :] = turn(x, 16 * level + 8 + dc)


def rims(got1, got2, even, block, lane):
    first = (lane & 8) == 0
    res = []
    for pair in range(5):
        if pair < 4:
            row, second = 128 * (pair // 2) + 16 * block, pair % 2 == 1
        else:
            row, second = 256 + 16 * (block % 4), block >= 4
        one, two = got1[row : row + 16, :], got2[row : row + 16, :]
        from_east = jnp.where(even, one, two)
        from_west = jnp.where(even, two, one)
        if second:
            from_west, from_east = turn(from_west, -8), turn(from_east, 8)
        res.append(jnp.where(first, from_west, from_east))
    return res


def tiles_of(main, rim_tiles, block, lane, which):
    rows = slice(16 * block, 16 * block + 16)
    res = []
    for v, dc in which:
        at = v if v < 9 else 10 + dc
        rim = turn(rim_tiles[v // 2], dc + 64 * (v % 2))
        res.append(join([main[at, level, rows, :] for level in range(LEVELS)], rim, dc, lane))
    return res


COEFS = [(c, dc_of(c)) for c in range(9)]


def pack_lat(main, got1, got2, pay1, pay2):
    lat = lax.axis_index("lat")
    even_lon = lax.axis_index("lon") % 2 == 0
    even = lat % 2 == 0
    is_top = lat == lax.axis_size("lat") - 1
    lane = lanes(16)
    which = COEFS + [(9, 0)]
    low = tiles_of(main, rims(got1, got2, even_lon, 0, lane), 0, lane, which)
    high = tiles_of(main, rims(got1, got2, even_lon, 7, lane), 7, lane, which)
    for v in range(10):
        for tile in range(TILES):
            south, north = low[v][tile][:8], high[v][tile][8:]
            pay1[v, tile] = jnp.where(even, north, south)
            pay2[v, tile] = jnp.where(even, south, north)

    @pl.when(is_top)
    def _():
        lane8, row8 = lanes(8), sublanes(8)
        for v in range(10):
            for tile in range(TILES):
                x = high[v][tile][8:]
                index = (lane8 ^ 15) if tile == LEVELS else ((143 + 32 * tile - lane8) & 127)
                x = jnp.take_along_axis(x, index, axis=1, mode="promise_in_bounds")
                x = jnp.take_along_axis(x, 7 - row8, axis=0, mode="promise_in_bounds")
                pay2[8 - v if v < 9 else 9, tile] = x


def sums(coef_tiles, field_tiles):
    res = []
    for dr in range(3):
        total = coef_tiles(3 * dr) * field_tiles[0]
        for dc in (1, 2):
            total = total + coef_tiles(3 * dr + dc) * field_tiles[dc]
        res.append(total)
    return res


def north_of(before, here, row):
    x = turn(here, 1, 0)
    return x if before is None else jnp.where(row == 0, turn(before, 1, 0), x)


def south_of(here, after, row):
    x = turn(here, -1, 0)
    return x if after is None else jnp.where(row == 7, turn(after, -1, 0), x)


def inner(main, got1, got2, wet, token, edge_coef, edge_field, saved, result, edge_wet, coef, field):
    del token
    even_lon = lax.axis_index("lon") % 2 == 0
    lane16 = lanes(16)
    for block in range(8):
        rows = slice(16 * block, 16 * block + 16)
        rim_tiles = rims(got1, got2, even_lon, block, lane16)
        built = tiles_of(main, rim_tiles, block, lane16, COEFS + [(9, -1), (9, 0), (9, 1)])
        for v in range(12):
            for tile in range(TILES):
                x = built[v][tile]
                if v < 9:
                    coef[v, tile, rows, :] = x
                else:
                    field[v - 9, tile, rows, :] = x
                if block in (0, 7):
                    side, part = (0, x[:8]) if block == 0 else (1, x[8:])
                    if v < 9:
                        edge_coef[v, side, tile] = part
                    else:
                        edge_field[v - 9, side, tile] = part
    for level in range(LEVELS):
        edge_wet[0, level] = wet[level, :8, :].astype(F32)
        edge_wet[1, level] = wet[level, SIZE - 8 :, :].astype(F32)

    lane, row = lanes(8), sublanes(8)

    def step(k, last):
        done = [None] * TILES
        older = [[None] * TILES, [None] * TILES]
        for t in range(17):
            now = []
            for tile in range(TILES):
                if t < 16:
                    rows = slice(8 * t, 8 * t + 8)
                    now.append(sums(lambda c: coef[c, tile, rows, :], [field[dc, tile, rows, :] for dc in range(3)]))
            if t < 16:
                for tile in range(TILES):
                    if t == 1:
                        saved[k, 0, tile] = now[tile][0]
                    if t == 14:
                        saved[k, 1, tile] = now[tile][2]
            if t >= 1 and not (last and t - 1 in (0, 15)):
                new = []
                for tile in range(TILES):
                    after = now[tile][0] if t < 16 else None
                    new.append(done[tile] + south_of(older[0][tile], after, row))
                rows = slice(8 * (t - 1), 8 * t)
                if last:
                    for level in range(LEVELS):
                        mask = wet[level, rows, :].astype(F32)
                        result[level, rows, :] = mask * turn(new[level], -(16 * level + 8))
                else:
                    for dc in (-1, 0, 1):
                        for tile, x in enumerate(new if dc == 0 else shifted(new, dc, lane)):
                            field[dc + 1, tile, rows, :] = x
            if t < 16:
                for tile in range(TILES):
                    done[tile] = now[tile][1] + north_of(older[1][tile], now[tile][2], row)
                    older[0][tile], older[1][tile] = now[tile][0], now[tile][2]

    lax.fori_loop(0, STEPS - 1, lambda k, _: (step(k, False), 0)[1], 0)
    step(STEPS - 1, True)


def finish(edge_coef, edge_field, saved, result, edge_wet, got1, got2, out, field, halo):
    even = lax.axis_index("lat") % 2 == 0
    lane, row = lanes(8), sublanes(8)
    for level in range(LEVELS):
        out[level, 8 : SIZE - 8, :] = result[level, 8 : SIZE - 8, :]
    for v in range(10):
        for tile in range(TILES):
            one, two = got1[v, tile], got2[v, tile]
            halo[v, 0, tile] = jnp.where(even, two, one)
            halo[v, 1, tile] = jnp.where(even, one, two)
    for side in range(2):
        tiles = [halo[9, side, tile] for tile in range(TILES)]
        for dc in (-1, 0, 1):
            for tile, x in enumerate(tiles if dc == 0 else shifted(tiles, dc, lane)):
                field[dc + 1, 3 * side, tile] = x
            for tile in range(TILES):
                field[dc + 1, 1 + side, tile] = edge_field[dc + 1, side, tile]

    for k in range(STEPS):
        new = [[], [], [], []]
        for tile in range(TILES):
            now = []
            for place in range(4):
                if place in (0, 3):
                    get = lambda c: halo[c, place // 3, tile]
                else:
                    get = lambda c: edge_coef[c, place - 1, tile]
                now.append(sums(get, [field[dc, place, tile] for dc in range(3)]))
            for place in range(4):
                before = (None, now[0][2], saved[k, 1, tile], now[2][2])[place]
                after = (now[1][0], saved[k, 0, tile], now[3][0], None)[place]
                new[place].append(
                    now[place][1] + north_of(before, now[place][2], row) + south_of(now[place][0], after, row)
                )
        if k < STEPS - 1:
            for place in range(4):
                for dc in (-1, 0, 1):
                    for tile, x in enumerate(new[place] if dc == 0 else shifted(new[place], dc, lane)):
                        field[dc + 1, place, tile] = x
        else:
            for side in range(2):
                rows = slice(0, 8) if side == 0 else slice(SIZE - 8, SIZE)
                for level in range(LEVELS):
                    x = turn(new[1 + side][level], -(16 * level + 8))
                    out[level, rows, :] = edge_wet[side, level] * x


VMEM = pl.BlockSpec(memory_space=pltpu.VMEM)


def call(body, args, outs, scratch=(), flops=1000000, near=True):
    kind = pltpu.VMEM if near else jax.ShapeDtypeStruct
    return pl.pallas_call(
        body,
        out_shape=[kind(shape, F32) for shape in outs],
        in_specs=[VMEM] * len(args),
        out_specs=[VMEM] * len(outs),
        scratch_shapes=[pltpu.VMEM(shape, F32) for shape in scratch],
        compiler_params=pltpu.CompilerParams(vmem_limit_bytes=40 * 1024 * 1024),
        cost_estimate=pl.CostEstimate(flops=flops, bytes_accessed=4 * 1024 * 1024, transcendentals=0),
        name=body.__name__,
    )(*args)


def shards(cotangent, coefficients, wet_mask):
    num_lon, num_lat = lax.axis_size("lon"), lax.axis_size("lat")

    def swap_lon(x, odd):
        pairs = [(i, ((i + odd) ^ 1) - odd) for i in range(num_lon)]
        return lax.ppermute(x, "lon", [(i, j % num_lon) for i, j in pairs])

    def swap_chip(x):
        return lax.ppermute(x, "lat", [(i, i ^ 1) for i in range(num_lat)])

    def swap_far(x):
        pairs = []
        for lon in range(num_lon):
            for lat in range(1, num_lat - 1):
                pairs.append((lon * num_lat + lat, lon * num_lat + ((lat + 1) ^ 1) - 1))
            pairs.append((lon * num_lat + num_lat - 1, (num_lon - 1 - lon) * num_lat + num_lat - 1))
        return lax.ppermute(x, ("lon", "lat"), pairs)

    fields = (cotangent, coefficients, wet_mask)
    lon1, lon2 = call(pack_lon, fields, [(320, SIZE)] * 2)
    got2 = swap_lon(lon2, 1)
    got1 = swap_lon(lon1, 0)
    main = call(rotate_main, fields + (lon1,), [(12, LEVELS, SIZE, SIZE)])[0]
    lat1, lat2 = call(pack_lat, (main, got1, got2), [(10, TILES, 8, SIZE)] * 2)
    far2 = swap_far(lat2)
    far1 = swap_chip(lat1)
    held = call(
        inner,
        (main, got1, got2, wet_mask, lat1),
        [(9, 2, TILES, 8, SIZE), (3, 2, TILES, 8, SIZE), (STEPS, 2, TILES, 8, SIZE), (LEVELS, SIZE, SIZE), (2, LEVELS, 8, SIZE)],
        [(9, TILES, SIZE, SIZE), (3, TILES, SIZE, SIZE)],
        flops=30000000,
    )
    return call(
        finish,
        tuple(held) + (far1, far2),
        [(LEVELS, SIZE, SIZE)],
        [(3, 4, TILES, 8, SIZE), (10, 2, TILES, 8, SIZE)],
        near=False,
    )[0]


def solution(mesh):
    in_specs = (P(None, "lat", "lon"), P(None, None, "lat", "lon"), P(None, "lat", "lon"))
    out_specs = P(None, "lat", "lon")
    return jax.shard_map(shards, mesh=mesh, in_specs=in_specs, out_specs=out_specs, check_vma=False)
```

time: 588 us -> 45 us (0.08)
  the two profiles are of different devices: /device:TPU:80 before, /device:TPU:1 now
where the time goes in v1:
time: 45 us; the launch traced here: 44.7 us
  starting transfers between devices  29.3 us (65%)
  Pallas kernels  8.39 us (19%)
  waiting for transfers between devices  3.83 us (9%)
  local copies, waits for them, and re-layouts  3.17 us (7%)
    ppermute x2, starting transfers between devices, swap_lon(): return lax.ppermute(x, 'lon', [(i, j % num_lon) for i, j in pairs])  16.5 us
    ppermute x1, starting transfers between devices, swap_far(): return lax.ppermute(x, ('lon', 'lat'), pairs)  10.9 us
    pallas_call x5, Pallas kernels, call(): pl.pallas_call(body, out_shape=[kind(shape, F32) for shape in outs], in_s...  8.39 us
    ppermute x2, waiting for transfers between devices, swap_lon(): return lax.ppermute(x, 'lon', [(i, j % num_lon) for i, j in pairs])  3.83 us
    unnamed x6, local copies, waits for them, and re-layouts  3.17 us
    ppermute x1, starting transfers between devices, swap_chip(): return lax.ppermute(x, 'lat', [(i, i ^ 1) for i in range(num_lat)])  1.92 us
  transfers between devices with their start and end apart: 4, of which 2 were waited for; matrix products, arithmetic and copies ran while one was open for 0% of the time, Pallas kernels for 10%

profile of v1, /device:TPU:1, one launch (start us, length us, event | category | flops | bytes accessed | tf_op | source)
XLA Modules:
  0.0 44.7 jit_solution(12513258109260790262)
XLA Ops:
  0.0 0.0 copy-start
  0.0 1.3 %copy-done = bf16[9,4,128,128]{3,2,1,0:T(8,128)(2,1)S(1)} copy-done((bf16[9,4,128,128]{3,2,1,0:T(8,128)(2,1)S(1)}, bf16[9,4,128,128]{3,2,1,0:T(8,128)(2,1)}, u32[]{:S(2)}) %copy-start) | copy-done | bytes 1179672
  1.3 0.0 copy-start.1
  1.3 0.9 %copy-done.1 = s32[4,128,128]{2,1,0:T(8,128)S(1)} copy-done((s32[4,128,128]{2,1,0:T(8,128)S(1)}, s32[4,128,128]{2,1,0:T(8,128)}, u32[]{:S(2)}) %copy-start.1) | copy-done | bytes 262168
  2.2 0.0 copy-start.2
  2.2 0.9 %copy-done.2 = f32[4,128,128]{2,1,0:T(8,128)S(1)} copy-done((f32[4,128,128]{2,1,0:T(8,128)S(1)}, f32[4,128,128]{2,1,0:T(8,128)}, u32[]{:S(2)}) %copy-start.2) | copy-done | bytes 262168
  3.2 2.0 %pack_lon.1 = (f32[320,128]{1,0:T(8,128)S(1)}, f32[320,128]{1,0:T(8,128)S(1)}) custom-call(f32[4,128,128]{2,1,0:T(8,128)S(1)} %copy-done.2, bf16[9,4,128,128]{3,2,1,0:T(8,128)(2,1)S(1)} %copy-done, s32[4,128,128]{2,1,0:T(8,128)S(1)} %copy-done.1), custom_call_target="tpu_custom_call" | custom-call | flops 1000000 | bytes 4194304 | tf_op jit(solution)/shard_map/pack_lon/pallas_call | solution.py:300
  5.1 14.5 %collective-permute-start.1 = (f32[320,128]{1,0:T(8,128)S(1)}, f32[320,128]{1,0:T(8,128)S(1)}, u32[]{:S(2)}, u32[]{:S(2)}) collective-permute-start(f32[320,128]{1,0:T(8,128)S(1)} %get-tuple-element.15), channel_id=1, source_target_pairs={{0,496},{16,32},{32,16},{48,64},{64,48},{80,96},{96,80},{112,128},... | collective-permute-start | bytes 491528 | tf_op jit(solution)/shard_map/ppermute | solution.py:317
  19.7 1.9 %collective-permute-start = (f32[320,128]{1,0:T(8,128)S(1)}, f32[320,128]{1,0:T(8,128)S(1)}, u32[]{:S(2)}, u32[]{:S(2)}) collective-permute-start(f32[320,128]{1,0:T(8,128)S(1)} %get-tuple-element.14.token), channel_id=1, source_target_pairs={{0,16},{16,0},{32,48},{48,32},{64,80},{80,64},{96,112},{112,96},{1... | collective-permute-start | bytes 491528 | tf_op jit(solution)/shard_map/ppermute | solution.py:317
  21.6 0.9 %rotate_main.1.main = f32[12,4,128,128]{3,2,1,0:T(8,128)S(1)} custom-call(f32[4,128,128]{2,1,0:T(8,128)S(1)} %copy-done.2, bf16[9,4,128,128]{3,2,1,0:T(8,128)(2,1)S(1)} %copy-done, s32[4,128,128]{2,1,0:T(8,128)S(1)} %copy-done.1, f32[320,128]{1,0:T(8,128)S(1)} %get-tuple-element.14.token), custom_call_target="tpu_custom_call" | custom-call | flops 1000000 | bytes 4194304 | tf_op jit(solution)/shard_map/rotate_main/pallas_call | solution.py:300
  22.5 1.1 %collective-permute-done.1.got2 = f32[320,128]{1,0:T(8,128)S(1)} collective-permute-done((f32[320,128]{1,0:T(8,128)S(1)}, f32[320,128]{1,0:T(8,128)S(1)}, u32[]{:S(2)}, u32[]{:S(2)}) %collective-permute-start.1) | collective-permute-done | bytes 163872 | tf_op jit(solution)/shard_map/ppermute | solution.py:317
  23.6 2.7 %collective-permute-done.got1 = f32[320,128]{1,0:T(8,128)S(1)} collective-permute-done((f32[320,128]{1,0:T(8,128)S(1)}, f32[320,128]{1,0:T(8,128)S(1)}, u32[]{:S(2)}, u32[]{:S(2)}) %collective-permute-start) | collective-permute-done | bytes 163872 | tf_op jit(solution)/shard_map/ppermute | solution.py:317
  26.3 0.2 pack_lat.1
  26.5 10.9 %collective-permute-start.3 = (f32[10,5,8,128]{3,2,1,0:T(8,128)S(1)}, f32[10,5,8,128]{3,2,1,0:T(8,128)S(1)}, u32[]{:S(2)}, u32[]{:S(2)}) collective-permute-start(f32[10,5,8,128]{3,2,1,0:T(8,128)S(1)} %get-tuple-element.22), channel_id=1, source_target_pairs={{1,2},{2,1},{3,4},{4,3},{5,6},{6,5},{7,8},{8,7},{9,10},{10,9},{11,... | collective-permute-start | bytes 614408 | tf_op jit(solution)/shard_map/ppermute | solution.py:328
  37.4 1.9 %collective-permute-start.2 = (f32[10,5,8,128]{3,2,1,0:T(8,128)S(1)}, f32[10,5,8,128]{3,2,1,0:T(8,128)S(1)}, u32[]{:S(2)}, u32[]{:S(2)}) collective-permute-start(f32[10,5,8,128]{3,2,1,0:T(8,128)S(1)} %get-tuple-element.16.token), channel_id=1, source_target_pairs={{0,1},{1,0},{2,3},{3,2},{4,5},{5,4},{6,7},{7,6},{8,9},{9,8},{10,11... | collective-permute-start | bytes 614408 | tf_op jit(solution)/shard_map/ppermute | solution.py:320
  39.3 3.5 %inner.1 = (f32[9,2,5,8,128]{4,3,2,1,0:T(8,128)S(1)}, f32[3,2,5,8,128]{4,3,2,1,0:T(8,128)S(1)}, f32[8,2,5,8,128]{4,3,2,1,0:T(8,128)S(1)}, f32[4,128,128]{2,1,0:T(8,128)S(1)}, f32[2,4,8,128]{3,2,1,0:T(8,128)S(1)}) custom-call(f32[12,4,128,128]{3,2,1,0:T(8,128)S(1)} %rotate_main.1.main, f32[320,128]{1,0:T(8,128)S(1)} %collective-permute-done.got1, ...), custom_call_target="tpu_custom_call" | custom-call | flops 30000000 | bytes 4194304 | tf_op jit(solution)/shard_map/inner/pallas_call | solution.py:300
  42.8 0.0 collective-permute-done.3.got2
  42.8 0.0 collective-permute-done.2.got1
  42.9 1.9 %finish.1 = f32[4,128,128]{2,1,0:T(8,128)} custom-call(f32[9,2,5,8,128]{4,3,2,1,0:T(8,128)S(1)} %get-tuple-element.17.edge_coef, f32[3,2,5,8,128]{4,3,2,1,0:T(8,128)S(1)} %get-tuple-element.18.edge_field, f32[8,2,5,8,128]{4,3,2,1,0:T(8,128)S(1)} %get-tuple-element.19.saved, f32[4,128,128]{2,1,0:T(8,128)S(1)} %get-tuple-element.20.result, ...), custom_call_target="tpu_custom_call" | custom-call | flops 1000000 | bytes 4194304 | tf_op jit(solution)/shard_map/finish/pallas_call | solution.py:300
Async XLA Ops:
  0.0 1.3 %copy-start = (bf16[9,4,128,128]{3,2,1,0:T(8,128)(2,1)S(1)}, bf16[9,4,128,128]{3,2,1,0:T(8,128)(2,1)}, u32[]{:S(2)}) copy-start(bf16[9,4,128,128]{3,2,1,0:T(8,128)(2,1)} %coef.3) | copy-start | bytes 3538948
  1.3 0.9 %copy-start.1 = (s32[4,128,128]{2,1,0:T(8,128)S(1)}, s32[4,128,128]{2,1,0:T(8,128)}, u32[]{:S(2)}) copy-start(s32[4,128,128]{2,1,0:T(8,128)} %wet.5) | copy-start | bytes 786436
  2.2 0.9 %copy-start.2 = (f32[4,128,128]{2,1,0:T(8,128)S(1)}, f32[4,128,128]{2,1,0:T(8,128)}, u32[]{:S(2)}) copy-start(f32[4,128,128]{2,1,0:T(8,128)} %cot.3) | copy-start | bytes 786436
  5.1 18.5 %collective-permute-start.1 = (f32[320,128]{1,0:T(8,128)S(1)}, f32[320,128]{1,0:T(8,128)S(1)}, u32[]{:S(2)}, u32[]{:S(2)}) collective-permute-start(f32[320,128]{1,0:T(8,128)S(1)} %get-tuple-element.15), channel_id=1, source_target_pairs={{0,496},{16,32},{32,16},{48,64},{64,48},{80,96},{96,80},{112,128},... | collective-permute-start | bytes 491528 | tf_op jit(solution)/shard_map/ppermute | solution.py:317
  19.7 6.6 %collective-permute-start = (f32[320,128]{1,0:T(8,128)S(1)}, f32[320,128]{1,0:T(8,128)S(1)}, u32[]{:S(2)}, u32[]{:S(2)}) collective-permute-start(f32[320,128]{1,0:T(8,128)S(1)} %get-tuple-element.14.token), channel_id=1, source_target_pairs={{0,16},{16,0},{32,48},{48,32},{64,80},{80,64},{96,112},{112,96},{1... | collective-permute-start | bytes 491528 | tf_op jit(solution)/shard_map/ppermute | solution.py:317
  26.5 16.3 %collective-permute-start.3 = (f32[10,5,8,128]{3,2,1,0:T(8,128)S(1)}, f32[10,5,8,128]{3,2,1,0:T(8,128)S(1)}, u32[]{:S(2)}, u32[]{:S(2)}) collective-permute-start(f32[10,5,8,128]{3,2,1,0:T(8,128)S(1)} %get-tuple-element.22), channel_id=1, source_target_pairs={{1,2},{2,1},{3,4},{4,3},{5,6},{6,5},{7,8},{8,7},{9,10},{10,9},{11,... | collective-permute-start | bytes 614408 | tf_op jit(solution)/shard_map/ppermute | solution.py:328
  37.4 5.4 %collective-permute-start.2 = (f32[10,5,8,128]{3,2,1,0:T(8,128)S(1)}, f32[10,5,8,128]{3,2,1,0:T(8,128)S(1)}, u32[]{:S(2)}, u32[]{:S(2)}) collective-permute-start(f32[10,5,8,128]{3,2,1,0:T(8,128)S(1)} %get-tuple-element.16.token), channel_id=1, source_target_pairs={{0,1},{1,0},{2,3},{3,2},{4,5},{5,4},{6,7},{7,6},{8,9},{9,8},{10,11... | collective-permute-start | bytes 614408 | tf_op jit(solution)/shard_map/ppermute | solution.py:320

commit v2 on v1

v2 whole, which is shorter than its diff:
```python
import jax
import jax.numpy as jnp
from jax import lax
from jax.experimental import pallas as pl
from jax.experimental.pallas import tpu as pltpu
from jax.sharding import PartitionSpec as P


STEPS = 8
LEVELS = 4
SIZE = 128
TILES = LEVELS + 1
F32 = jnp.float32
BF16 = jnp.bfloat16


def dc_of(c):
    return c % 3 - 1


def lanes(rows):
    return lax.broadcasted_iota(jnp.int32, (rows, SIZE), 1)


def sublanes(rows):
    return lax.broadcasted_iota(jnp.int32, (rows, SIZE), 0)


def turn(x, shift, axis=1):
    shift = shift % x.shape[axis]
    return x if shift == 0 else pltpu.roll(x, shift, axis)


def seam(level, dc):
    return 16 * level + (8 if dc == 1 else 7)


def join(mains, rim, dc, lane):
    if dc == 0:
        return list(mains) + [rim]
    fixed, new_rim = [], rim
    for level in range(LEVELS):
        here = lane == seam(level, dc)
        fixed.append(jnp.where(here, rim, mains[level]))
        new_rim = jnp.where(here, mains[level], new_rim)
    return fixed + [new_rim]


def shifted(tiles, dc, lane):
    return join([turn(t, dc) for t in tiles[:LEVELS]], turn(tiles[LEVELS], dc), dc, lane)


def edge_choices(choose):
    choose[...] = jnp.zeros_like(choose)
    cell, lane = sublanes(16), lanes(16)
    for block in range(16):
        value, level = block // LEVELS, block % LEVELS
        base = 64 * (value % 2) + 16 * level
        second = value >= 2
        at = lane - (base + (8 if second else 0))
        east = (cell >= 8) & (cell - 8 == at)
        at = lane - (base + (0 if second else 8))
        west = (cell < 8) & (cell == at)
        choose[SIZE * block + SIZE - 16 : SIZE * block + SIZE, :SIZE] = east.astype(F32).astype(BF16)
        choose[SIZE * block : SIZE * block + 16, SIZE:] = west.astype(F32).astype(BF16)


def column(v, level):
    return slice(SIZE * (LEVELS * v + level), SIZE * (LEVELS * v + level) + SIZE)


def pack_lon(cot_far, coef_far, wet_far, pay1, pay2, masked, cot, wet, coef, choose, sems):
    parts = [(0, 4), (4, 8), (8, 9)]
    copies = [pltpu.make_async_copy(wet_far, wet, sems.at[0])]
    for n, (start, stop) in enumerate(parts):
        copies.append(pltpu.make_async_copy(coef_far.at[start:stop], coef.at[start:stop], sems.at[1 + n]))
    copies.append(pltpu.make_async_copy(cot_far, cot, sems.at[4]))
    for copy in copies:
        copy.start()
    is_top = lax.axis_index("lat") == lax.axis_size("lat") - 1
    edge_choices(choose)

    copies[0].wait()
    sea = [wet[level].astype(F32).astype(BF16) for level in range(LEVELS)]
    for n, (start, stop) in enumerate(parts):
        copies[1 + n].wait()
        for v in range(start, stop):
            for level in range(LEVELS):
                masked[:, column(v, level)] = coef[v, level] * sea[level]
                if v >= 6:
                    rows = slice(SIZE - 16, SIZE)
                    here, other = coef[v, level, rows, :].astype(F32), coef[8 - v, level, rows, :].astype(F32)
                    here = jnp.where((sublanes(16) == 15) & is_top, other, here)
                    masked[rows, column(v, level)] = (here * wet[level, rows, :].astype(F32)).astype(BF16)
        if n < 2:
            both = jnp.dot(masked[:, 2048 * n : 2048 * n + 2048], choose[...], preferred_element_type=F32)
            east, west = both[:, :SIZE], both[:, SIZE:]
            pay1[SIZE * n : SIZE * n + SIZE, :] = east
            pay2[SIZE * n : SIZE * n + SIZE, :] = west

    lane = lanes(16)
    first = (lane & 8) == 0

    def both_edges(block):
        out = None
        for half in (0, 1):
            for level in range(LEVELS):
                rows = slice(16 * block, 16 * block + 16)
                x = cot[level, rows, :] if half else masked[rows, column(8, level)].astype(F32)
                x = turn(x, 64 * half + 16 * level + 8)
                out = x if out is None else jnp.where((lane >> 4) == 4 * half + level, x, out)
        return out

    copies[4].wait()
    for block in range(4):
        a, b = both_edges(block), both_edges(block + 4)
        row = 256 + 16 * block
        pay1[row : row + 16, :] = jnp.where(first, a, turn(b, 8))
        pay2[row : row + 16, :] = jnp.where(first, turn(b, -8), a)


def rotate_main(masked, cot, token, out):
    del token
    for block in range(8):
        rows = slice(16 * block, 16 * block + 16)
        for level in range(LEVELS):
            for v in range(9):
                out[v, level, rows, :] = turn(masked[rows, column(v, level)].astype(F32), 16 * level + 8 + dc_of(v))
            for dc in (-1, 0, 1):
                out[10 + dc, level, rows, :] = turn(cot[level, rows, :], 16 * level + 8 + dc)


def rims(got1, got2, start, count, lane):
    first = (lane & 8) == 0
    res = []
    for pair in range(5):
        if pair < 4:
            row, second = SIZE * (pair // 2) + start, pair % 2 == 1
        else:
            row, second = 256 + start % 64, start >= 64
        from_west, from_east = got1[row : row + count, :], got2[row : row + count, :]
        if second:
            from_west, from_east = turn(from_west, -8), turn(from_east, 8)
        res.append(jnp.where(first, from_west, from_east))
    return res


VALUES = [(c, dc_of(c)) for c in range(9)] + [(9, -1), (9, 0), (9, 1)]


def tiles_of(main, got1, got2, start, count, lane):
    rim_tiles = rims(got1, got2, start, count, lane)
    rows = slice(start, start + count)
    res = []
    for v, dc in VALUES:
        at = v if v < 9 else 10 + dc
        rim = turn(rim_tiles[v // 2], dc + 64 * (v % 2))
        res.append(join([main[at, level, rows, :] for level in range(LEVELS)], rim, dc, lane))
    return res


PAIRS = [(0, 1), (2, 3), (4, None), (8, 7), (6, 5)]
MIRRORED = [3, 4, 2, 0, 1, 5]
SENT = 27


def outgoing(built, northward, lane, row):
    near = (row >= 4) if northward else (row < 4)
    units = []
    for one, two in PAIRS:
        if two is None:
            units.append(built[one])
        else:
            units.append([jnp.where(near, built[one][t], turn(built[two][t], 4, 0)) for t in range(TILES)])
    field, added = built[9:], [jnp.zeros((8, SIZE), F32)] * TILES
    for k in range(4):
        new = []
        for t in range(TILES):
            down, level, up = sums(lambda c: built[c][t], [field[dc][t] for dc in range(3)])
            up, down = turn(up, 1, 0), turn(down, -1, 0)
            across = up if northward else down
            if northward:
                place_a, place_b = (0 if k == 0 else 4 - k), 7 - k
            else:
                place_a, place_b = (7 if k == 0 else k + 3), k
            a = across if k == 0 else turn(across, 4, 0)
            added[t] = jnp.where(row == place_a, a, jnp.where(row == place_b, level + across, added[t]))
            new.append(level + up + down)
        if k < 3:
            field = [shifted(new, -1, lane), new, shifted(new, 1, lane)]
    return units + [added]


def pack_lat(main, got1, got2, pay1, pay2):
    lat = lax.axis_index("lat")
    even = lat % 2 == 0
    is_top = lat == lax.axis_size("lat") - 1
    lane, row = lanes(8), sublanes(8)
    south = outgoing(tiles_of(main, got1, got2, 0, 8, lane), False, lane, row)
    north = outgoing(tiles_of(main, got1, got2, SIZE - 8, 8, lane), True, lane, row)

    def flat(units):
        res = [units[u][t] for u in range(6) for t in range(LEVELS)]
        return res + [jnp.where(lane < 64, units[u][LEVELS], turn(units[u + 1][LEVELS], 64)) for u in (0, 2, 4)]

    south_flat, north_flat = flat(south), flat(north)
    for n in range(SENT):
        pay1[n] = jnp.where(even, north_flat[n], south_flat[n])
        pay2[n] = jnp.where(even, south_flat[n], north_flat[n])

    @pl.when(is_top)
    def _():
        turned = [None] * 6
        for u in range(6):
            tiles = []
            for tile in range(TILES):
                index = (lane ^ 15) if tile == LEVELS else ((143 + 32 * tile - lane) & 127)
                x = jnp.take_along_axis(north[u][tile], index, axis=1, mode="promise_in_bounds")
                tiles.append(jnp.take_along_axis(x, 7 - row, axis=0, mode="promise_in_bounds"))
            turned[MIRRORED[u]] = tiles
        for n, x in enumerate(flat(turned)):
            pay2[n] = x


def sums(coef_tiles, field_tiles):
    res = []
    for dr in range(3):
        total = coef_tiles(3 * dr) * field_tiles[0]
        for dc in (1, 2):
            total = total + coef_tiles(3 * dr + dc) * field_tiles[dc]
        res.append(total)
    return res


def north_of(before, here, row):
    x = turn(here, 1, 0)
    return x if before is None else jnp.where(row == 0, turn(before, 1, 0), x)


def south_of(here, after, row):
    x = turn(here, -1, 0)
    return x if after is None else jnp.where(row == 7, turn(after, -1, 0), x)


def inner(main, got1, got2, wet, token, edge_coef, edge_field, saved, result, edge_wet, coef, field):
    del token
    lane16 = lanes(16)
    for block in range(8):
        rows = slice(16 * block, 16 * block + 16)
        built = tiles_of(main, got1, got2, 16 * block, 16, lane16)
        for v in range(12):
            for tile in range(TILES):
                x = built[v][tile]
                if v < 9:
                    coef[v, tile, rows, :] = x
                else:
                    field[v - 9, tile, rows, :] = x
                if block in (0, 7):
                    side, part = (0, x[:8]) if block == 0 else (1, x[8:])
                    if v < 9:
                        edge_coef[v, side, tile] = part
                    else:
                        edge_field[v - 9, side, tile] = part
    for level in range(LEVELS):
        edge_wet[0, level] = wet[level, :8, :].astype(F32)
        edge_wet[1, level] = wet[level, SIZE - 8 :, :].astype(F32)

    lane, row = lanes(8), sublanes(8)

    def step(k, last):
        done = [None] * TILES
        older = [[None] * TILES, [None] * TILES]
        for t in range(17):
            now = []
            for tile in range(TILES):
                if t < 16:
                    rows = slice(8 * t, 8 * t + 8)
                    now.append(sums(lambda c: coef[c, tile, rows, :], [field[dc, tile, rows, :] for dc in range(3)]))
            if t < 16:
                for tile in range(TILES):
                    if t == 1:
                        saved[k, 0, tile] = now[tile][0]
                    if t == 14:
                        saved[k, 1, tile] = now[tile][2]
            if t >= 1 and not (last and t - 1 in (0, 15)):
                new = []
                for tile in range(TILES):
                    after = now[tile][0] if t < 16 else None
                    new.append(done[tile] + south_of(older[0][tile], after, row))
                rows = slice(8 * (t - 1), 8 * t)
                if last:
                    for level in range(LEVELS):
                        mask = wet[level, rows, :].astype(F32)
                        result[level, rows, :] = mask * turn(new[level], -(16 * level + 8))
                else:
                    for dc in (-1, 0, 1):
                        for tile, x in enumerate(new if dc == 0 else shifted(new, dc, lane)):
                            field[dc + 1, tile, rows, :] = x
            if t < 16:
                for tile in range(TILES):
                    done[tile] = now[tile][1] + north_of(older[1][tile], now[tile][2], row)
                    older[0][tile], older[1][tile] = now[tile][0], now[tile][2]

    lax.fori_loop(0, STEPS - 1, lambda k, _: (step(k, False), 0)[1], 0)
    step(STEPS - 1, True)


def finish(edge_coef, edge_field, saved, result, edge_wet, got1, got2, out, field, halo, added):
    even = lax.axis_index("lat") % 2 == 0
    lane, row = lanes(8), sublanes(8)
    for level in range(LEVELS):
        out[level, 8 : SIZE - 8, :] = result[level, 8 : SIZE - 8, :]
    for side in range(2):
        near = (row >= 4) if side == 0 else (row < 4)
        got = [jnp.where(even, got2[n], got1[n]) if side == 0 else jnp.where(even, got1[n], got2[n]) for n in range(SENT)]
        for u in range(6):
            for tile in range(TILES):
                if tile < LEVELS:
                    x = got[LEVELS * u + tile]
                else:
                    x = turn(got[24 + u // 2], 64 * (u % 2))
                if u == 5:
                    added[side, tile] = x
                else:
                    one, two = PAIRS[u]
                    halo[one, side, tile] = jnp.where(near, x, 0.0)
                    if two is not None:
                        halo[two, side, tile] = jnp.where(near, turn(x, 4, 0), 0.0)
        for dc in range(3):
            for tile in range(TILES):
                field[dc, 1 + side, tile] = edge_field[dc, side, tile]

    zero = jnp.zeros((8, SIZE), F32)
    for k in range(STEPS):
        new = [[], [], [], []]
        for tile in range(TILES):
            now = []
            for place in range(4):
                if place in (0, 3):
                    get = lambda c: halo[c, place // 3, tile]
                else:
                    get = lambda c: edge_coef[c, place - 1, tile]
                if k == 0 and place in (0, 3):
                    now.append([zero] * 3)
                else:
                    now.append(sums(get, [field[dc, place, tile] for dc in range(3)]))
            total = []
            for place in range(4):
                before = (None, now[0][2], saved[k, 1, tile], now[2][2])[place]
                after = (now[1][0], saved[k, 0, tile], now[3][0], None)[place]
                total.append(now[place][1] + north_of(before, now[place][2], row) + south_of(now[place][0], after, row))
            if k < 4:
                low, high = added[0, tile], added[1, tile]
                total[0] = total[0] + jnp.where(row == 7 - k, low, 0.0)
                total[3] = total[3] + jnp.where(row == k, high, 0.0)
                if k == 0:
                    total[1] = total[1] + jnp.where(row == 0, low, 0.0)
                    total[2] = total[2] + jnp.where(row == 7, high, 0.0)
                else:
                    total[0] = total[0] + jnp.where(row == 8 - k, turn(low, 4, 0), 0.0)
                    total[3] = total[3] + jnp.where(row == k - 1, turn(high, 4, 0), 0.0)
            for place in range(4):
                new[place].append(total[place])
        if k < STEPS - 1:
            for place in range(4):
                for dc in (-1, 0, 1):
                    for tile, x in enumerate(new[place] if dc == 0 else shifted(new[place], dc, lane)):
                        field[dc + 1, place, tile] = x
        else:
            for side in range(2):
                rows = slice(0, 8) if side == 0 else slice(SIZE - 8, SIZE)
                for level in range(LEVELS):
                    x = turn(new[1 + side][level], -(16 * level + 8))
                    out[level, rows, :] = edge_wet[side, level] * x


VMEM = pl.BlockSpec(memory_space=pltpu.VMEM)


def call(body, args, outs, scratch=(), flops=1000000, near=True, far_args=False):
    kind = pltpu.VMEM if near else jax.ShapeDtypeStruct
    return pl.pallas_call(
        body,
        out_shape=[kind(*(out if isinstance(out[0], tuple) else (out, F32))) for out in outs],
        in_specs=[pl.BlockSpec(memory_space=pl.ANY) if far_args else VMEM] * len(args),
        out_specs=[VMEM] * len(outs),
        scratch_shapes=[pltpu.VMEM(shape, F32) if isinstance(shape, tuple) else shape for shape in scratch],
        compiler_params=pltpu.CompilerParams(vmem_limit_bytes=40 * 1024 * 1024),
        cost_estimate=pl.CostEstimate(flops=flops, bytes_accessed=4 * 1024 * 1024, transcendentals=0),
        name=body.__name__,
    )(*args)


def shards(cotangent, coefficients, wet_mask):
    num_lon, num_lat = lax.axis_size("lon"), lax.axis_size("lat")

    def shift_lon(x, by):
        return lax.ppermute(x, "lon", [(i, (i + by) % num_lon) for i in range(num_lon)])

    def swap_chip(x):
        return lax.ppermute(x, "lat", [(i, i ^ 1) for i in range(num_lat)])

    def swap_far(x):
        pairs = []
        for lon in range(num_lon):
            for lat in range(1, num_lat - 1):
                pairs.append((lon * num_lat + lat, lon * num_lat + ((lat + 1) ^ 1) - 1))
            pairs.append((lon * num_lat + num_lat - 1, (num_lon - 1 - lon) * num_lat + num_lat - 1))
        return lax.ppermute(x, ("lon", "lat"), pairs)

    fields = [pltpu.with_memory_space_constraint(x, pltpu.HBM) for x in (cotangent, coefficients, wet_mask)]
    whole = (LEVELS, SIZE, SIZE)
    lon1, lon2, masked, cot, wet = call(
        pack_lon,
        fields,
        [(320, SIZE), (320, SIZE), ((SIZE, 36 * SIZE), BF16), whole, (whole, jnp.int32)],
        [pltpu.VMEM((9,) + whole, BF16), pltpu.VMEM((16 * SIZE, 2 * SIZE), BF16), pltpu.SemaphoreType.DMA((5,))],
        far_args=True,
    )
    got1 = shift_lon(lon1, 1)
    got2 = shift_lon(lon2, -1)
    main = call(rotate_main, (masked, cot, lon1), [(12,) + whole])[0]
    lat1, lat2 = call(pack_lat, (main, got1, got2), [(SENT, 8, SIZE)] * 2)
    far2 = swap_far(lat2)
    far1 = swap_chip(lat1)
    held = call(
        inner,
        (main, got1, got2, wet, lat2),
        [(9, 2, TILES, 8, SIZE), (3, 2, TILES, 8, SIZE), (STEPS, 2, TILES, 8, SIZE), whole, (2, LEVELS, 8, SIZE)],
        [(9, TILES, SIZE, SIZE), (3, TILES, SIZE, SIZE)],
        flops=30000000,
    )
    return call(
        finish,
        tuple(held) + (far1, far2),
        [whole],
        [(3, 4, TILES, 8, SIZE), (9, 2, TILES, 8, SIZE), (2, TILES, 8, SIZE)],
        near=False,
    )[0]


def solution(mesh):
    in_specs = (P(None, "lat", "lon"), P(None, None, "lat", "lon"), P(None, "lat", "lon"))
    out_specs = P(None, "lat", "lon")
    return jax.shard_map(shards, mesh=mesh, in_specs=in_specs, out_specs=out_specs, check_vma=False)
```

time: 45 us -> 36.2 us (0.80)
  starting transfers between devices: 29.3 us -> 24.6 us
  local copies, waits for them, and re-layouts: 3.17 us -> 0 us
  waiting for transfers between devices: 3.83 us -> 2.27 us
    ppermute x1, starting transfers between devices: 10.9 us -> 6.18 us  [swap_far(): return lax.ppermute(x, ('lon', 'lat'), pairs)]
    unnamed x6 -> x0, local copies, waits for them, and re-layouts: 3.17 us -> none
    ppermute x2, waiting for transfers between devices: 3.83 us -> 2.27 us  [shift_lon(): lax.ppermute(x, 'lon', [(i, (i + by) % num_lon) for i in range(num_lon)])]
  transfers between devices with their start and end apart: 4 -> 4, of which waited for: 2 -> 2; matrix products, arithmetic and copies ran while one was open for 0% -> 0% of each run, Pallas kernels for 10% -> 12%
where the time goes in v2:
time: 36.2 us; the launch traced here: 35.6 us
  starting transfers between devices  24.6 us (68%)
  Pallas kernels  8.75 us (24%)
  waiting for transfers between devices  2.27 us (6%)
    ppermute x2, starting transfers between devices, shift_lon(): lax.ppermute(x, 'lon', [(i, (i + by) % num_lon) for i in range(num_lon)])  16.5 us
    pallas_call x5, Pallas kernels, call(): pl.pallas_call(body, out_shape=[kind(*(out if isinstance(out[0], tuple) e...  8.75 us
    ppermute x1, starting transfers between devices, swap_far(): return lax.ppermute(x, ('lon', 'lat'), pairs)  6.18 us
    ppermute x2, waiting for transfers between devices, shift_lon(): lax.ppermute(x, 'lon', [(i, (i + by) % num_lon) for i in range(num_lon)])  2.27 us
    ppermute x1, starting transfers between devices, swap_chip(): return lax.ppermute(x, 'lat', [(i, i ^ 1) for i in range(num_lat)])  1.92 us
  transfers between devices with their start and end apart: 4, of which 2 were waited for; matrix products, arithmetic and copies ran while one was open for 0% of the time, Pallas kernels for 12%

profile of v2, /device:TPU:1, one launch (start us, length us, event | category | flops | bytes accessed | tf_op | source)
XLA Modules:
  0.0 35.6 jit_solution(5216104020180598446)
XLA Ops:
  0.0 2.3 %pack_lon.1 = (f32[320,128]{1,0:T(8,128)S(1)}, f32[320,128]{1,0:T(8,128)S(1)}, bf16[128,4608]{1,0:T(8,128)(2,1)S(1)}, f32[4,128,128]{2,1,0:T(8,128)S(1)}, s32[4,128,128]{2,1,0:T(8,128)S(1)}) custom-call(f32[4,128,128]{2,1,0:T(8,128)} %cot_far.1, bf16[9,4,128,128]{3,2,1,0:T(8,128)(2,1)} %coef_far.1, s32[4,128,128]{2,1,0:T(8,128)} %wet_far.1), custom_call_target="tpu_custom_call" | custom-call | flops 1000000 | bytes 4194304 | tf_op jit(solution)/shard_map/pack_lon/pallas_call | solution.py:382
  2.3 4.0 %collective-permute-start = (f32[320,128]{1,0:T(8,128)S(1)}, f32[320,128]{1,0:T(8,128)S(1)}, u32[]{:S(2)}, u32[]{:S(2)}) collective-permute-start(f32[320,128]{1,0:T(8,128)S(1)} %get-tuple-element.19.token), channel_id=1, source_target_pairs={{0,16},{16,32},{32,48},{48,64},{64,80},{80,96},{96,112},{112,128},... | collective-permute-start | bytes 491528 | tf_op jit(solution)/shard_map/ppermute | solution.py:398
  6.4 12.4 %collective-permute-start.1 = (f32[320,128]{1,0:T(8,128)S(1)}, f32[320,128]{1,0:T(8,128)S(1)}, u32[]{:S(2)}, u32[]{:S(2)}) collective-permute-start(f32[320,128]{1,0:T(8,128)S(1)} %get-tuple-element.20), channel_id=1, source_target_pairs={{0,496},{16,0},{32,16},{48,32},{64,48},{80,64},{96,80},{112,96},{1... | collective-permute-start | bytes 491528 | tf_op jit(solution)/shard_map/ppermute | solution.py:398
  18.8 0.6 %rotate_main.1.main = f32[12,4,128,128]{3,2,1,0:T(8,128)S(1)} custom-call(bf16[128,4608]{1,0:T(8,128)(2,1)S(1)} %get-tuple-element.17.masked, f32[4,128,128]{2,1,0:T(8,128)S(1)} %get-tuple-element.18.cot, f32[320,128]{1,0:T(8,128)S(1)} %get-tuple-element.19.token), custom_call_target="tpu_custom_call" | custom-call | flops 1000000 | bytes 4194304 | tf_op jit(solution)/shard_map/rotate_main/pallas_call | solution.py:382
  19.4 1.4 %collective-permute-done.got1 = f32[320,128]{1,0:T(8,128)S(1)} collective-permute-done((f32[320,128]{1,0:T(8,128)S(1)}, f32[320,128]{1,0:T(8,128)S(1)}, u32[]{:S(2)}, u32[]{:S(2)}) %collective-permute-start) | collective-permute-done | bytes 163872 | tf_op jit(solution)/shard_map/ppermute | solution.py:398
  20.8 0.9 %collective-permute-done.1.got2 = f32[320,128]{1,0:T(8,128)S(1)} collective-permute-done((f32[320,128]{1,0:T(8,128)S(1)}, f32[320,128]{1,0:T(8,128)S(1)}, u32[]{:S(2)}, u32[]{:S(2)}) %collective-permute-start.1) | collective-permute-done | bytes 163872 | tf_op jit(solution)/shard_map/ppermute | solution.py:398
  21.6 0.6 %pack_lat.1 = (f32[27,8,128]{2,1,0:T(8,128)S(1)}, f32[27,8,128]{2,1,0:T(8,128)S(1)}) custom-call(f32[12,4,128,128]{3,2,1,0:T(8,128)S(1)} %rotate_main.1.main, f32[320,128]{1,0:T(8,128)S(1)} %collective-permute-done.got1, f32[320,128]{1,0:T(8,128)S(1)} %collective-permute-done.1.got2), custom_call_target="tpu_custom_call" | custom-call | flops 1000000 | bytes 4194304 | tf_op jit(solution)/shard_map/pack_lat/pallas_call | solution.py:382
  22.2 6.2 %collective-permute-start.3 = (f32[27,8,128]{2,1,0:T(8,128)S(1)}, f32[27,8,128]{2,1,0:T(8,128)S(1)}, u32[]{:S(2)}, u32[]{:S(2)}) collective-permute-start(f32[27,8,128]{2,1,0:T(8,128)S(1)} %get-tuple-element.22.token), channel_id=1, source_target_pairs={{1,2},{2,1},{3,4},{4,3},{5,6},{6,5},{7,8},{8,7},{9,10},{10,9},{11,... | collective-permute-start | bytes 331784 | tf_op jit(solution)/shard_map/ppermute | solution.py:409
  28.4 1.9 %collective-permute-start.2 = (f32[27,8,128]{2,1,0:T(8,128)S(1)}, f32[27,8,128]{2,1,0:T(8,128)S(1)}, u32[]{:S(2)}, u32[]{:S(2)}) collective-permute-start(f32[27,8,128]{2,1,0:T(8,128)S(1)} %get-tuple-element.28), channel_id=1, source_target_pairs={{0,1},{1,0},{2,3},{3,2},{4,5},{5,4},{6,7},{7,6},{8,9},{9,8},{10,11... | collective-permute-start | bytes 331784 | tf_op jit(solution)/shard_map/ppermute | solution.py:401
  30.3 3.5 %inner.1 = (f32[9,2,5,8,128]{4,3,2,1,0:T(8,128)S(1)}, f32[3,2,5,8,128]{4,3,2,1,0:T(8,128)S(1)}, f32[8,2,5,8,128]{4,3,2,1,0:T(8,128)S(1)}, f32[4,128,128]{2,1,0:T(8,128)S(1)}, f32[2,4,8,128]{3,2,1,0:T(8,128)S(1)}) custom-call(f32[12,4,128,128]{3,2,1,0:T(8,128)S(1)} %rotate_main.1.main, f32[320,128]{1,0:T(8,128)S(1)} %collective-permute-done.got1, ...), custom_call_target="tpu_custom_call" | custom-call | flops 30000000 | bytes 4194304 | tf_op jit(solution)/shard_map/inner/pallas_call | solution.py:382
  33.8 0.0 collective-permute-done.3.got2
  33.9 0.0 collective-permute-done.2.got1
  33.9 1.8 %finish.1 = f32[4,128,128]{2,1,0:T(8,128)} custom-call(f32[9,2,5,8,128]{4,3,2,1,0:T(8,128)S(1)} %get-tuple-element.23.edge_coef, f32[3,2,5,8,128]{4,3,2,1,0:T(8,128)S(1)} %get-tuple-element.24.edge_field, f32[8,2,5,8,128]{4,3,2,1,0:T(8,128)S(1)} %get-tuple-element.25.saved, f32[4,128,128]{2,1,0:T(8,128)S(1)} %get-tuple-element.26.result, ...), custom_call_target="tpu_custom_call" | custom-call | flops 1000000 | bytes 4194304 | tf_op jit(solution)/shard_map/finish/pallas_call | solution.py:382
Async XLA Ops:
  2.3 18.5 %collective-permute-start = (f32[320,128]{1,0:T(8,128)S(1)}, f32[320,128]{1,0:T(8,128)S(1)}, u32[]{:S(2)}, u32[]{:S(2)}) collective-permute-start(f32[320,128]{1,0:T(8,128)S(1)} %get-tuple-element.19.token), channel_id=1, source_target_pairs={{0,16},{16,32},{32,48},{48,64},{64,80},{80,96},{96,112},{112,128},... | collective-permute-start | bytes 491528 | tf_op jit(solution)/shard_map/ppermute | solution.py:398
  6.4 15.3 %collective-permute-start.1 = (f32[320,128]{1,0:T(8,128)S(1)}, f32[320,128]{1,0:T(8,128)S(1)}, u32[]{:S(2)}, u32[]{:S(2)}) collective-permute-start(f32[320,128]{1,0:T(8,128)S(1)} %get-tuple-element.20), channel_id=1, source_target_pairs={{0,496},{16,0},{32,16},{48,32},{64,48},{80,64},{96,80},{112,96},{1... | collective-permute-start | bytes 491528 | tf_op jit(solution)/shard_map/ppermute | solution.py:398
  22.2 11.7 %collective-permute-start.3 = (f32[27,8,128]{2,1,0:T(8,128)S(1)}, f32[27,8,128]{2,1,0:T(8,128)S(1)}, u32[]{:S(2)}, u32[]{:S(2)}) collective-permute-start(f32[27,8,128]{2,1,0:T(8,128)S(1)} %get-tuple-element.22.token), channel_id=1, source_target_pairs={{1,2},{2,1},{3,4},{4,3},{5,6},{6,5},{7,8},{8,7},{9,10},{10,9},{11,... | collective-permute-start | bytes 331784 | tf_op jit(solution)/shard_map/ppermute | solution.py:409
  28.4 5.5 %collective-permute-start.2 = (f32[27,8,128]{2,1,0:T(8,128)S(1)}, f32[27,8,128]{2,1,0:T(8,128)S(1)}, u32[]{:S(2)}, u32[]{:S(2)}) collective-permute-start(f32[27,8,128]{2,1,0:T(8,128)S(1)} %get-tuple-element.28), channel_id=1, source_target_pairs={{0,1},{1,0},{2,3},{3,2},{4,5},{5,4},{6,7},{7,6},{8,9},{9,8},{10,11... | collective-permute-start | bytes 331784 | tf_op jit(solution)/shard_map/ppermute | solution.py:401

commit v3 on v2

--- a/solution.py
+++ b/solution.py
@@ -50,19 +50,39 @@
     return join([turn(t, dc) for t in tiles[:LEVELS]], turn(tiles[LEVELS], dc), dc, lane)
 
 
-def edge_choices(choose):
+EAST_LENT = [((0, 1), 0, (0, 1)), ((2, 3), 3, (0, 1)), ((4, 5), 6, (0, 1)), ((6,), 1, (0,)), ((7,), 4, (0,))]
+WEST_LENT = [((0, 1), 2, (6, 7)), ((2, 3), 5, (6, 7)), ((4,), 1, (7,)), ((5,), 4, (7,))]
+
+
+def place(c, level, eastward):
+    second = (c % 4 >= 2) == eastward
+    return 64 * (c % 2) + 16 * level + (8 if second else 0)
+
+
+def edge_choices(choose, part):
     choose[...] = jnp.zeros_like(choose)
     cell, lane = sublanes(16), lanes(16)
-    for block in range(16):
+    for block in range(5 * LEVELS):
         value, level = block // LEVELS, block % LEVELS
-        base = 64 * (value % 2) + 16 * level
-        second = value >= 2
-        at = lane - (base + (8 if second else 0))
-        east = (cell >= 8) & (cell - 8 == at)
-        at = lane - (base + (0 if second else 8))
-        west = (cell < 8) & (cell == at)
-        choose[SIZE * block + SIZE - 16 : SIZE * block + SIZE, :SIZE] = east.astype(F32).astype(BF16)
-        choose[SIZE * block : SIZE * block + 16, SIZE:] = west.astype(F32).astype(BF16)
+        for eastward in (True, False):
+            lent = EAST_LENT if eastward else WEST_LENT
+            x = cell - 8 if eastward else cell
+            hit = None
+            if value < 4:
+                c = 4 * part + value
+                taken = [t for _, host, cells in lent if host == c for t in cells]
+                hit = (x == lane - place(c, level, eastward)) & (x >= 0) & (x < 8)
+                for t in taken:
+                    hit = hit & (x != t)
+            else:
+                for cells, host, at in lent:
+                    if host // 4 == part:
+                        for one, t in zip(cells, at):
+                            here = (x == one) & (lane == place(host, level, eastward) + t)
+                            hit = here if hit is None else hit | here
+            start = SIZE * block + (SIZE - 16 if eastward else 0)
+            columns = slice(0, SIZE) if eastward else slice(SIZE, 2 * SIZE)
+            choose[start : start + 16, columns] = hit.astype(F32).astype(BF16)
 
 
 def column(v, level):
@@ -70,7 +90,7 @@
 
 
 def pack_lon(cot_far, coef_far, wet_far, pay1, pay2, masked, cot, wet, coef, choose, sems):
-    parts = [(0, 4), (4, 8), (8, 9)]
+    parts = [(8, 9), (0, 4), (4, 8)]
     copies = [pltpu.make_async_copy(wet_far, wet, sems.at[0])]
     for n, (start, stop) in enumerate(parts):
         copies.append(pltpu.make_async_copy(coef_far.at[start:stop], coef.at[start:stop], sems.at[1 + n]))
@@ -78,7 +98,8 @@
     for copy in copies:
         copy.start()
     is_top = lax.axis_index("lat") == lax.axis_size("lat") - 1
-    edge_choices(choose)
+    for part in range(2):
+        edge_choices(choose.at[part], part)
 
     copies[0].wait()
     sea = [wet[level].astype(F32).astype(BF16) for level in range(LEVELS)]
@@ -87,34 +108,34 @@
         for v in range(start, stop):
             for level in range(LEVELS):
                 masked[:, column(v, level)] = coef[v, level] * sea[level]
-                if v >= 6:
-                    rows = slice(SIZE - 16, SIZE)
-                    here, other = coef[v, level, rows, :].astype(F32), coef[8 - v, level, rows, :].astype(F32)
-                    here = jnp.where((sublanes(16) == 15) & is_top, other, here)
-                    masked[rows, column(v, level)] = (here * wet[level, rows, :].astype(F32)).astype(BF16)
-        if n < 2:
-            both = jnp.dot(masked[:, 2048 * n : 2048 * n + 2048], choose[...], preferred_element_type=F32)
-            east, west = both[:, :SIZE], both[:, SIZE:]
-            pay1[SIZE * n : SIZE * n + SIZE, :] = east
-            pay2[SIZE * n : SIZE * n + SIZE, :] = west
+        if n == 2:
+            copies[4].wait()
+        for v in range(6, 9) if n == 2 else ():
+            for level in range(LEVELS):
+                rows = slice(SIZE - 16, SIZE)
+                here, other = coef[v, level, rows, :].astype(F32), coef[8 - v, level, rows, :].astype(F32)
+                here = jnp.where((sublanes(16) == 15) & is_top, other, here)
+                masked[rows, column(v, level)] = (here * wet[level, rows, :].astype(F32)).astype(BF16)
+    for part in range(2):
+        both = jnp.dot(masked[:, 2048 * part : 2048 * part + 2048], choose[part, :2048], preferred_element_type=F32)
+        both = both + jnp.dot(masked[:, 4096:], choose[part, 2048:], preferred_element_type=F32)
+        pay1[SIZE * part : SIZE * part + SIZE, :] = both[:, :SIZE]
+        pay2[SIZE * part : SIZE * part + SIZE, :] = both[:, SIZE:]
 
     lane = lanes(16)
     first = (lane & 8) == 0
 
-    def both_edges(block):
+    def both_edges(start):
         out = None
-        for half in (0, 1):
-            for level in range(LEVELS):
-                rows = slice(16 * block, 16 * block + 16)
-                x = cot[level, rows, :] if half else masked[rows, column(8, level)].astype(F32)
-                x = turn(x, 64 * half + 16 * level + 8)
-                out = x if out is None else jnp.where((lane >> 4) == 4 * half + level, x, out)
+        for level in range(LEVELS):
+            x = turn(cot[level, start : start + 16, :], 16 * level + 8)
+            out = x if out is None else jnp.where((lane >> 4) == level, x, out)
         return out
 
-    copies[4].wait()
-    for block in range(4):
-        a, b = both_edges(block), both_edges(block + 4)
-        row = 256 + 16 * block
+    for half in range(2):
+        a, b, c, d = [both_edges(32 * n + 16 * half) for n in range(4)]
+        a, b = jnp.where(lane < 64, a, turn(c, 64)), jnp.where(lane < 64, b, turn(d, 64))
+        row = 256 + 16 * half
         pay1[row : row + 16, :] = jnp.where(first, a, turn(b, 8))
         pay2[row : row + 16, :] = jnp.where(first, turn(b, -8), a)
 
@@ -132,17 +153,25 @@
 
 def rims(got1, got2, start, count, lane):
     first = (lane & 8) == 0
+    parts = [(got1[row : row + count, :], got2[row : row + count, :]) for row in (start, SIZE + start)]
     res = []
-    for pair in range(5):
-        if pair < 4:
-            row, second = SIZE * (pair // 2) + start, pair % 2 == 1
-        else:
-            row, second = 256 + start % 64, start >= 64
-        from_west, from_east = got1[row : row + count, :], got2[row : row + count, :]
-        if second:
+    for pair in range(4):
+        from_west, from_east = parts[pair // 2]
+        if pair % 2 == 1:
             from_west, from_east = turn(from_west, -8), turn(from_east, 8)
         res.append(jnp.where(first, from_west, from_east))
-    return res
+    row, n = 256 + start % 32, start // 32
+    shift = 64 - 64 * (n // 2)
+    from_west = turn(got1[row : row + count, :], shift - 8 * (n % 2))
+    from_east = turn(got2[row : row + count, :], shift + 8 * (n % 2))
+    last = jnp.where(first, from_west, from_east)
+    for side, lent in ((0, EAST_LENT), (1, WEST_LENT)):
+        for cells, host, at in lent:
+            target = cells[0] + 8 * side
+            x = turn(parts[host // 4][side], target - place(host, 0, side == 0) - at[0])
+            within = (lane & 15) - target
+            last = jnp.where((lane < 64) & (within >= 0) & (within < len(cells)), x, last)
+    return res + [last]
 
 
 VALUES = [(c, dc_of(c)) for c in range(9)] + [(9, -1), (9, 0), (9, 1)]
@@ -159,19 +188,30 @@
     return res
 
 
-PAIRS = [(0, 1), (2, 3), (4, None), (8, 7), (6, 5)]
-MIRRORED = [3, 4, 2, 0, 1, 5]
-SENT = 27
+PAIRS = [(0, 1), (2, 3), (8, 7), (6, 5)]
+MIRRORED = [2, 3, 0, 1, 4]
+MIDDLE = {True: [(1, 0, True), (2, 0, False), (3, 1, True)], False: [(1, 2, True), (2, 2, False), (3, 3, True)]}
+UNITS = 5
+SENT = 23
+
+
+def ring_row(ring, northward):
+    return 8 - ring if northward else ring - 1
+
+
+def middle_row(near, northward):
+    return (ring_row(4, northward) + (0 if near else 4)) % 8
 
 
 def outgoing(built, northward, lane, row):
     near = (row >= 4) if northward else (row < 4)
     units = []
     for one, two in PAIRS:
-        if two is None:
-            units.append(built[one])
-        else:
-            units.append([jnp.where(near, built[one][t], turn(built[two][t], 4, 0)) for t in range(TILES)])
+        units.append([jnp.where(near, built[one][t], turn(built[two][t], 4, 0)) for t in range(TILES)])
+    for ring, u, in_near in MIDDLE[northward]:
+        at = middle_row(in_near, northward)
+        for t in range(TILES):
+            units[u][t] = jnp.where(row == at, turn(built[4][t], at - ring_row(ring, northward), 0), units[u][t])
     field, added = built[9:], [jnp.zeros((8, SIZE), F32)] * TILES
     for k in range(4):
         new = []
@@ -200,8 +240,9 @@
     north = outgoing(tiles_of(main, got1, got2, SIZE - 8, 8, lane), True, lane, row)
 
     def flat(units):
-        res = [units[u][t] for u in range(6) for t in range(LEVELS)]
-        return res + [jnp.where(lane < 64, units[u][LEVELS], turn(units[u + 1][LEVELS], 64)) for u in (0, 2, 4)]
+        res = [units[u][t] for u in range(UNITS) for t in range(LEVELS)]
+        rim = [unit[LEVELS] for unit in units]
+        return res + [jnp.where(lane < 64, rim[0], turn(rim[1], 64)), jnp.where(lane < 64, rim[2], turn(rim[3], 64)), rim[4]]
 
     south_flat, north_flat = flat(south), flat(north)
     for n in range(SENT):
@@ -210,8 +251,8 @@
 
     @pl.when(is_top)
     def _():
-        turned = [None] * 6
-        for u in range(6):
+        turned = [None] * UNITS
+        for u in range(UNITS):
             tiles = []
             for tile in range(TILES):
                 index = (lane ^ 15) if tile == LEVELS else ((143 + 32 * tile - lane) & 127)
@@ -233,16 +274,14 @@
 
 
 def north_of(before, here, row):
-    x = turn(here, 1, 0)
-    return x if before is None else jnp.where(row == 0, turn(before, 1, 0), x)
+    return turn(here if before is None else jnp.where(row == 7, before, here), 1, 0)
 
 
 def south_of(here, after, row):
-    x = turn(here, -1, 0)
-    return x if after is None else jnp.where(row == 7, turn(after, -1, 0), x)
-
-
-def inner(main, got1, got2, wet, token, edge_coef, edge_field, saved, result, edge_wet, coef, field):
+    return turn(here if after is None else jnp.where(row == 0, after, here), -1, 0)
+
+
+def inner(main, got1, got2, wet, token, edge_coef, edge_field, saved, result, edge_wet, coef, field, other):
     del token
     lane16 = lanes(16)
     for block in range(8):
@@ -252,7 +291,8 @@
             for tile in range(TILES):
                 x = built[v][tile]
                 if v < 9:
-                    coef[v, tile, rows, :] = x
+                    if dc_of(v) != 0 or tile == LEVELS:
+                        coef[v, tile, rows, :] = x
                 else:
                     field[v - 9, tile, rows, :] = x
                 if block in (0, 7):
@@ -267,7 +307,10 @@
 
     lane, row = lanes(8), sublanes(8)
 
-    def step(k, last):
+    def weight(c, tile, rows):
+        return main[c, tile, rows, :] if dc_of(c) == 0 and tile < LEVELS else coef[c, tile, rows, :]
+
+    def step(k, last, field, other):
         done = [None] * TILES
         older = [[None] * TILES, [None] * TILES]
         for t in range(17):
@@ -275,7 +318,7 @@
             for tile in range(TILES):
                 if t < 16:
                     rows = slice(8 * t, 8 * t + 8)
-                    now.append(sums(lambda c: coef[c, tile, rows, :], [field[dc, tile, rows, :] for dc in range(3)]))
+                    now.append(sums(lambda c: weight(c, tile, rows), [field[dc, tile, rows, :] for dc in range(3)]))
             if t < 16:
                 for tile in range(TILES):
                     if t == 1:
@@ -295,14 +338,20 @@
                 else:
                     for dc in (-1, 0, 1):
                         for tile, x in enumerate(new if dc == 0 else shifted(new, dc, lane)):
-                            field[dc + 1, tile, rows, :] = x
+                            other[dc + 1, tile, rows, :] = x
             if t < 16:
                 for tile in range(TILES):
                     done[tile] = now[tile][1] + north_of(older[1][tile], now[tile][2], row)
                     older[0][tile], older[1][tile] = now[tile][0], now[tile][2]
 
-    lax.fori_loop(0, STEPS - 1, lambda k, _: (step(k, False), 0)[1], 0)
-    step(STEPS - 1, True)
+    def two_steps(n, carry):
+        step(2 * n, False, field, other)
+        step(2 * n + 1, False, other, field)
+        return carry
+
+    lax.fori_loop(0, STEPS // 2 - 1, two_steps, 0)
+    step(STEPS - 2, False, field, other)
+    step(STEPS - 1, True, other, field)
 
 
 def finish(edge_coef, edge_field, saved, result, edge_wet, got1, got2, out, field, halo, added):
@@ -313,19 +362,21 @@
     for side in range(2):
         near = (row >= 4) if side == 0 else (row < 4)
         got = [jnp.where(even, got2[n], got1[n]) if side == 0 else jnp.where(even, got1[n], got2[n]) for n in range(SENT)]
-        for u in range(6):
-            for tile in range(TILES):
-                if tile < LEVELS:
-                    x = got[LEVELS * u + tile]
-                else:
-                    x = turn(got[24 + u // 2], 64 * (u % 2))
-                if u == 5:
-                    added[side, tile] = x
-                else:
-                    one, two = PAIRS[u]
-                    halo[one, side, tile] = jnp.where(near, x, 0.0)
-                    if two is not None:
-                        halo[two, side, tile] = jnp.where(near, turn(x, 4, 0), 0.0)
+        northward = side == 0
+        for tile in range(TILES):
+            if tile < LEVELS:
+                units = [got[LEVELS * u + tile] for u in range(UNITS)]
+            else:
+                units = [turn(got[LEVELS * UNITS + u // 2], 64 * (u % 2)) for u in range(UNITS)]
+            added[side, tile] = units[4]
+            for u, (one, two) in enumerate(PAIRS):
+                halo[one, side, tile] = jnp.where(near, units[u], 0.0)
+                halo[two, side, tile] = jnp.where(near, turn(units[u], 4, 0), 0.0)
+            middle = jnp.zeros((8, SIZE), F32)
+            for ring, u, in_near in MIDDLE[northward]:
+                to = ring_row(ring, northward)
+                middle = jnp.where(row == to, turn(units[u], to - middle_row(in_near, northward), 0), middle)
+            halo[4, side, tile] = middle
         for dc in range(3):
             for tile in range(TILES):
                 field[dc, 1 + side, tile] = edge_field[dc, side, tile]
@@ -413,8 +464,8 @@
     lon1, lon2, masked, cot, wet = call(
         pack_lon,
         fields,
-        [(320, SIZE), (320, SIZE), ((SIZE, 36 * SIZE), BF16), whole, (whole, jnp.int32)],
-        [pltpu.VMEM((9,) + whole, BF16), pltpu.VMEM((16 * SIZE, 2 * SIZE), BF16), pltpu.SemaphoreType.DMA((5,))],
+        [(288, SIZE), (288, SIZE), ((SIZE, 36 * SIZE), BF16), whole, (whole, jnp.int32)],
+        [pltpu.VMEM((9,) + whole, BF16), pltpu.VMEM((2, 20 * SIZE, 2 * SIZE), BF16), pltpu.SemaphoreType.DMA((5,))],
         far_args=True,
     )
     got1 = shift_lon(lon1, 1)
@@ -427,7 +478,7 @@
         inner,
         (main, got1, got2, wet, lat2),
         [(9, 2, TILES, 8, SIZE), (3, 2, TILES, 8, SIZE), (STEPS, 2, TILES, 8, SIZE), whole, (2, LEVELS, 8, SIZE)],
-        [(9, TILES, SIZE, SIZE), (3, TILES, SIZE, SIZE)],
+        [(9, TILES, SIZE, SIZE), (3, TILES, SIZE, SIZE), (3, TILES, SIZE, SIZE)],
         flops=30000000,
     )
     return call(

time: 36.2 us -> 35.3 us (0.975); the launches traced: 35.6 us -> 35.1 us
  no operation moved by 1% of the time
where the time goes in v3:
time: 35.3 us; the launch traced here: 35.1 us
  starting transfers between devices  24.6 us (70%)
  Pallas kernels  8.57 us (24%)
  waiting for transfers between devices  1.91 us (5%)
    ppermute x2, starting transfers between devices, shift_lon(): lax.ppermute(x, 'lon', [(i, (i + by) % num_lon) for i in range(num_lon)])  16.4 us
    pallas_call x5, Pallas kernels, call(): pl.pallas_call(body, out_shape=[kind(*(out if isinstance(out[0], tuple) e...  8.57 us
    ppermute x1, starting transfers between devices, swap_far(): return lax.ppermute(x, ('lon', 'lat'), pairs)  6.2 us
    ppermute x1, starting transfers between devices, swap_chip(): return lax.ppermute(x, 'lat', [(i, i ^ 1) for i in range(num_lat)])  1.92 us
    ppermute x2, waiting for transfers between devices, shift_lon(): lax.ppermute(x, 'lon', [(i, (i + by) % num_lon) for i in range(num_lon)])  1.91 us
  transfers between devices with their start and end apart: 4, of which 2 were waited for; matrix products, arithmetic and copies ran while one was open for 0% of the time, Pallas kernels for 12%

profile of v3, /device:TPU:1, one launch (start us, length us, event | category | flops | bytes accessed | tf_op | source)
XLA Modules:
  0.0 35.1 jit_solution(35017740739021835)
XLA Ops:
  0.0 2.0 %pack_lon.1 = (f32[288,128]{1,0:T(8,128)S(1)}, f32[288,128]{1,0:T(8,128)S(1)}, bf16[128,4608]{1,0:T(8,128)(2,1)S(1)}, f32[4,128,128]{2,1,0:T(8,128)S(1)}, s32[4,128,128]{2,1,0:T(8,128)S(1)}) custom-call(f32[4,128,128]{2,1,0:T(8,128)} %cot_far.1, bf16[9,4,128,128]{3,2,1,0:T(8,128)(2,1)} %coef_far.1, s32[4,128,128]{2,1,0:T(8,128)} %wet_far.1), custom_call_target="tpu_custom_call" | custom-call | flops 1000000 | bytes 4194304 | tf_op jit(solution)/shard_map/pack_lon/pallas_call | solution.py:433
  2.0 4.0 %collective-permute-start = (f32[288,128]{1,0:T(8,128)S(1)}, f32[288,128]{1,0:T(8,128)S(1)}, u32[]{:S(2)}, u32[]{:S(2)}) collective-permute-start(f32[288,128]{1,0:T(8,128)S(1)} %get-tuple-element.19.token), channel_id=1, source_target_pairs={{0,16},{16,32},{32,48},{48,64},{64,80},{80,96},{96,112},{112,128},... | collective-permute-start | bytes 442376 | tf_op jit(solution)/shard_map/ppermute | solution.py:449
  6.1 12.4 %collective-permute-start.1 = (f32[288,128]{1,0:T(8,128)S(1)}, f32[288,128]{1,0:T(8,128)S(1)}, u32[]{:S(2)}, u32[]{:S(2)}) collective-permute-start(f32[288,128]{1,0:T(8,128)S(1)} %get-tuple-element.20), channel_id=1, source_target_pairs={{0,496},{16,0},{32,16},{48,32},{64,48},{80,64},{96,80},{112,96},{1... | collective-permute-start | bytes 442376 | tf_op jit(solution)/shard_map/ppermute | solution.py:449
  18.5 0.6 %rotate_main.1.main = f32[12,4,128,128]{3,2,1,0:T(8,128)S(1)} custom-call(bf16[128,4608]{1,0:T(8,128)(2,1)S(1)} %get-tuple-element.17.masked, f32[4,128,128]{2,1,0:T(8,128)S(1)} %get-tuple-element.18.cot, f32[288,128]{1,0:T(8,128)S(1)} %get-tuple-element.19.token), custom_call_target="tpu_custom_call" | custom-call | flops 1000000 | bytes 4194304 | tf_op jit(solution)/shard_map/rotate_main/pallas_call | solution.py:433
  19.1 1.0 %collective-permute-done.got1 = f32[288,128]{1,0:T(8,128)S(1)} collective-permute-done((f32[288,128]{1,0:T(8,128)S(1)}, f32[288,128]{1,0:T(8,128)S(1)}, u32[]{:S(2)}, u32[]{:S(2)}) %collective-permute-start) | collective-permute-done | bytes 147488 | tf_op jit(solution)/shard_map/ppermute | solution.py:449
  20.1 0.9 %collective-permute-done.1.got2 = f32[288,128]{1,0:T(8,128)S(1)} collective-permute-done((f32[288,128]{1,0:T(8,128)S(1)}, f32[288,128]{1,0:T(8,128)S(1)}, u32[]{:S(2)}, u32[]{:S(2)}) %collective-permute-start.1) | collective-permute-done | bytes 147488 | tf_op jit(solution)/shard_map/ppermute | solution.py:449
  21.0 0.5 %pack_lat.1 = (f32[23,8,128]{2,1,0:T(8,128)S(1)}, f32[23,8,128]{2,1,0:T(8,128)S(1)}) custom-call(f32[12,4,128,128]{3,2,1,0:T(8,128)S(1)} %rotate_main.1.main, f32[288,128]{1,0:T(8,128)S(1)} %collective-permute-done.got1, f32[288,128]{1,0:T(8,128)S(1)} %collective-permute-done.1.got2), custom_call_target="tpu_custom_call" | custom-call | flops 1000000 | bytes 4194304 | tf_op jit(solution)/shard_map/pack_lat/pallas_call | solution.py:433
  21.5 6.2 %collective-permute-start.3 = (f32[23,8,128]{2,1,0:T(8,128)S(1)}, f32[23,8,128]{2,1,0:T(8,128)S(1)}, u32[]{:S(2)}, u32[]{:S(2)}) collective-permute-start(f32[23,8,128]{2,1,0:T(8,128)S(1)} %get-tuple-element.22.token), channel_id=1, source_target_pairs={{1,2},{2,1},{3,4},{4,3},{5,6},{6,5},{7,8},{8,7},{9,10},{10,9},{11,... | collective-permute-start | bytes 282632 | tf_op jit(solution)/shard_map/ppermute | solution.py:460
  27.7 1.9 %collective-permute-start.2 = (f32[23,8,128]{2,1,0:T(8,128)S(1)}, f32[23,8,128]{2,1,0:T(8,128)S(1)}, u32[]{:S(2)}, u32[]{:S(2)}) collective-permute-start(f32[23,8,128]{2,1,0:T(8,128)S(1)} %get-tuple-element.28), channel_id=1, source_target_pairs={{0,1},{1,0},{2,3},{3,2},{4,5},{5,4},{6,7},{7,6},{8,9},{9,8},{10,11... | collective-permute-start | bytes 282632 | tf_op jit(solution)/shard_map/ppermute | solution.py:452
  29.6 3.7 %inner.1 = (f32[9,2,5,8,128]{4,3,2,1,0:T(8,128)S(1)}, f32[3,2,5,8,128]{4,3,2,1,0:T(8,128)S(1)}, f32[8,2,5,8,128]{4,3,2,1,0:T(8,128)S(1)}, f32[4,128,128]{2,1,0:T(8,128)S(1)}, f32[2,4,8,128]{3,2,1,0:T(8,128)S(1)}) custom-call(f32[12,4,128,128]{3,2,1,0:T(8,128)S(1)} %rotate_main.1.main, f32[288,128]{1,0:T(8,128)S(1)} %collective-permute-done.got1, ...), custom_call_target="tpu_custom_call" | custom-call | flops 30000000 | bytes 4194304 | tf_op jit(solution)/shard_map/inner/pallas_call | solution.py:433
  33.4 0.0 collective-permute-done.3.got2
  33.4 0.0 collective-permute-done.2.got1
  33.4 1.7 %finish.1 = f32[4,128,128]{2,1,0:T(8,128)} custom-call(f32[9,2,5,8,128]{4,3,2,1,0:T(8,128)S(1)} %get-tuple-element.23.edge_coef, f32[3,2,5,8,128]{4,3,2,1,0:T(8,128)S(1)} %get-tuple-element.24.edge_field, f32[8,2,5,8,128]{4,3,2,1,0:T(8,128)S(1)} %get-tuple-element.25.saved, f32[4,128,128]{2,1,0:T(8,128)S(1)} %get-tuple-element.26.result, ...), custom_call_target="tpu_custom_call" | custom-call | flops 1000000 | bytes 4194304 | tf_op jit(solution)/shard_map/finish/pallas_call | solution.py:433
Async XLA Ops:
  2.0 18.1 %collective-permute-start = (f32[288,128]{1,0:T(8,128)S(1)}, f32[288,128]{1,0:T(8,128)S(1)}, u32[]{:S(2)}, u32[]{:S(2)}) collective-permute-start(f32[288,128]{1,0:T(8,128)S(1)} %get-tuple-element.19.token), channel_id=1, source_target_pairs={{0,16},{16,32},{32,48},{48,64},{64,80},{80,96},{96,112},{112,128},... | collective-permute-start | bytes 442376 | tf_op jit(solution)/shard_map/ppermute | solution.py:449
  6.1 14.9 %collective-permute-start.1 = (f32[288,128]{1,0:T(8,128)S(1)}, f32[288,128]{1,0:T(8,128)S(1)}, u32[]{:S(2)}, u32[]{:S(2)}) collective-permute-start(f32[288,128]{1,0:T(8,128)S(1)} %get-tuple-element.20), channel_id=1, source_target_pairs={{0,496},{16,0},{32,16},{48,32},{64,48},{80,64},{96,80},{112,96},{1... | collective-permute-start | bytes 442376 | tf_op jit(solution)/shard_map/ppermute | solution.py:449
  21.5 11.9 %collective-permute-start.3 = (f32[23,8,128]{2,1,0:T(8,128)S(1)}, f32[23,8,128]{2,1,0:T(8,128)S(1)}, u32[]{:S(2)}, u32[]{:S(2)}) collective-permute-start(f32[23,8,128]{2,1,0:T(8,128)S(1)} %get-tuple-element.22.token), channel_id=1, source_target_pairs={{1,2},{2,1},{3,4},{4,3},{5,6},{6,5},{7,8},{8,7},{9,10},{10,9},{11,... | collective-permute-start | bytes 282632 | tf_op jit(solution)/shard_map/ppermute | solution.py:460
  27.7 5.7 %collective-permute-start.2 = (f32[23,8,128]{2,1,0:T(8,128)S(1)}, f32[23,8,128]{2,1,0:T(8,128)S(1)}, u32[]{:S(2)}, u32[]{:S(2)}) collective-permute-start(f32[23,8,128]{2,1,0:T(8,128)S(1)} %get-tuple-element.28), channel_id=1, source_target_pairs={{0,1},{1,0},{2,3},{3,2},{4,5},{5,4},{6,7},{7,6},{8,9},{9,8},{10,11... | collective-permute-start | bytes 282632 | tf_op jit(solution)/shard_map/ppermute | solution.py:452

commit v4 on v3

--- a/solution.py
+++ b/solution.py
@@ -274,7 +274,7 @@
 
 
 def north_of(before, here, row):
-    return turn(here if before is None else jnp.where(row == 7, before, here), 1, 0)
+    return turn(here if before is None else jnp.where(row == here.shape[0] - 1, before, here), 1, 0)
 
 
 def south_of(here, after, row):
@@ -305,32 +305,29 @@
         edge_wet[0, level] = wet[level, :8, :].astype(F32)
         edge_wet[1, level] = wet[level, SIZE - 8 :, :].astype(F32)
 
-    lane, row = lanes(8), sublanes(8)
+    lane, row = lane16, sublanes(16)
 
     def weight(c, tile, rows):
         return main[c, tile, rows, :] if dc_of(c) == 0 and tile < LEVELS else coef[c, tile, rows, :]
 
     def step(k, last, field, other):
-        done = [None] * TILES
-        older = [[None] * TILES, [None] * TILES]
-        for t in range(17):
+        done, older = [None] * TILES, [[None] * TILES, [None] * TILES]
+        for t in range(9):
             now = []
-            for tile in range(TILES):
-                if t < 16:
-                    rows = slice(8 * t, 8 * t + 8)
+            if t < 8:
+                rows = slice(16 * t, 16 * t + 16)
+                for tile in range(TILES):
                     now.append(sums(lambda c: weight(c, tile, rows), [field[dc, tile, rows, :] for dc in range(3)]))
-            if t < 16:
-                for tile in range(TILES):
-                    if t == 1:
-                        saved[k, 0, tile] = now[tile][0]
-                    if t == 14:
-                        saved[k, 1, tile] = now[tile][2]
-            if t >= 1 and not (last and t - 1 in (0, 15)):
+                    if t == 0:
+                        saved[k, 0, tile] = now[tile][0][8:]
+                    if t == 7:
+                        saved[k, 1, tile] = now[tile][2][:8]
+            if t >= 1:
                 new = []
                 for tile in range(TILES):
-                    after = now[tile][0] if t < 16 else None
+                    after = now[tile][0] if t < 8 else None
                     new.append(done[tile] + south_of(older[0][tile], after, row))
-                rows = slice(8 * (t - 1), 8 * t)
+                rows = slice(16 * (t - 1), 16 * t)
                 if last:
                     for level in range(LEVELS):
                         mask = wet[level, rows, :].astype(F32)
@@ -339,7 +336,7 @@
                     for dc in (-1, 0, 1):
                         for tile, x in enumerate(new if dc == 0 else shifted(new, dc, lane)):
                             other[dc + 1, tile, rows, :] = x
-            if t < 16:
+            if t < 8:
                 for tile in range(TILES):
                     done[tile] = now[tile][1] + north_of(older[1][tile], now[tile][2], row)
                     older[0][tile], older[1][tile] = now[tile][0], now[tile][2]
@@ -354,8 +351,10 @@
     step(STEPS - 1, True, other, field)
 
 
-def finish(edge_coef, edge_field, saved, result, edge_wet, got1, got2, out, field, halo, added):
-    even = lax.axis_index("lat") % 2 == 0
+def finish(edge_coef, edge_field, saved, result, edge_wet, both, got2, out, field, halo, added):
+    lat = lax.axis_index("lat")
+    even = lat % 2 == 0
+    got1 = both.at[1 - lat % 2]
     lane, row = lanes(8), sublanes(8)
     for level in range(LEVELS):
         out[level, 8 : SIZE - 8, :] = result[level, 8 : SIZE - 8, :]
@@ -449,7 +448,8 @@
         return lax.ppermute(x, "lon", [(i, (i + by) % num_lon) for i in range(num_lon)])
 
     def swap_chip(x):
-        return lax.ppermute(x, "lat", [(i, i ^ 1) for i in range(num_lat)])
+        pairs = [[i, i + 1] for i in range(0, num_lat, 2)]
+        return lax.all_gather(x, "lat", axis_index_groups=pairs)
 
     def swap_far(x):
         pairs = []

time: 35.3 us -> 35.2 us (level)
  starting transfers between devices: 24.6 us -> 22.6 us
  blocking collectives: 0 us -> 1.93 us
    all_gather x0 -> x1, blocking collectives: none -> 1.93 us  [swap_chip(): return lax.all_gather(x, 'lat', axis_index_groups=pairs)]
    ppermute x1 -> x0, starting transfers between devices: 1.92 us -> none  [swap_chip(): return lax.ppermute(x, 'lat', [(i, i ^ 1) for i in range(num_lat)])]
  transfers between devices with their start and end apart: 4 -> 3, of which waited for: 2 -> 2; matrix products, arithmetic and copies ran while one was open for 0% -> 0% of each run, Pallas kernels for 12% -> 12%
where the time goes in v4:
time: 35.2 us; the launch traced here: 35 us
  starting transfers between devices  22.6 us (64%)
  Pallas kernels  8.5 us (24%)
  blocking collectives  1.93 us (5%)
  waiting for transfers between devices  1.91 us (5%)
    ppermute x2, starting transfers between devices, shift_lon(): lax.ppermute(x, 'lon', [(i, (i + by) % num_lon) for i in range(num_lon)])  16.4 us
    pallas_call x5, Pallas kernels, call(): pl.pallas_call(body, out_shape=[kind(*(out if isinstance(out[0], tuple) e...  8.5 us
    ppermute x1, starting transfers between devices, swap_far(): return lax.ppermute(x, ('lon', 'lat'), pairs)  6.2 us
    all_gather x1, blocking collectives, swap_chip(): return lax.all_gather(x, 'lat', axis_index_groups=pairs)  1.93 us
    ppermute x2, waiting for transfers between devices, shift_lon(): lax.ppermute(x, 'lon', [(i, (i + by) % num_lon) for i in range(num_lon)])  1.91 us
  transfers between devices with their start and end apart: 3, of which 2 were waited for; matrix products, arithmetic and copies ran while one was open for 0% of the time, Pallas kernels for 12%

profile of v4, /device:TPU:1, one launch (start us, length us, event | category | flops | bytes accessed | tf_op | source)
XLA Modules:
  0.0 35.0 jit_solution(15913708512468616423)
XLA Ops:
  0.0 2.0 %pack_lon.1 = (f32[288,128]{1,0:T(8,128)S(1)}, f32[288,128]{1,0:T(8,128)S(1)}, bf16[128,4608]{1,0:T(8,128)(2,1)S(1)}, f32[4,128,128]{2,1,0:T(8,128)S(1)}, s32[4,128,128]{2,1,0:T(8,128)S(1)}) custom-call(f32[4,128,128]{2,1,0:T(8,128)} %cot_far.1, bf16[9,4,128,128]{3,2,1,0:T(8,128)(2,1)} %coef_far.1, s32[4,128,128]{2,1,0:T(8,128)} %wet_far.1), custom_call_target="tpu_custom_call" | custom-call | flops 1000000 | bytes 4194304 | tf_op jit(solution)/shard_map/pack_lon/pallas_call | solution.py:432
  2.0 4.0 %collective-permute-start = (f32[288,128]{1,0:T(8,128)S(1)}, f32[288,128]{1,0:T(8,128)S(1)}, u32[]{:S(2)}, u32[]{:S(2)}) collective-permute-start(f32[288,128]{1,0:T(8,128)S(1)} %get-tuple-element.19.token), channel_id=1, source_target_pairs={{0,16},{16,32},{32,48},{48,64},{64,80},{80,96},{96,112},{112,128},... | collective-permute-start | bytes 442376 | tf_op jit(solution)/shard_map/ppermute | solution.py:448
  6.1 12.4 %collective-permute-start.1 = (f32[288,128]{1,0:T(8,128)S(1)}, f32[288,128]{1,0:T(8,128)S(1)}, u32[]{:S(2)}, u32[]{:S(2)}) collective-permute-start(f32[288,128]{1,0:T(8,128)S(1)} %get-tuple-element.20), channel_id=1, source_target_pairs={{0,496},{16,0},{32,16},{48,32},{64,48},{80,64},{96,80},{112,96},{1... | collective-permute-start | bytes 442376 | tf_op jit(solution)/shard_map/ppermute | solution.py:448
  18.5 0.6 %rotate_main.1.main = f32[12,4,128,128]{3,2,1,0:T(8,128)S(1)} custom-call(bf16[128,4608]{1,0:T(8,128)(2,1)S(1)} %get-tuple-element.17.masked, f32[4,128,128]{2,1,0:T(8,128)S(1)} %get-tuple-element.18.cot, f32[288,128]{1,0:T(8,128)S(1)} %get-tuple-element.19.token), custom_call_target="tpu_custom_call" | custom-call | flops 1000000 | bytes 4194304 | tf_op jit(solution)/shard_map/rotate_main/pallas_call | solution.py:432
  19.1 1.0 %collective-permute-done.got1 = f32[288,128]{1,0:T(8,128)S(1)} collective-permute-done((f32[288,128]{1,0:T(8,128)S(1)}, f32[288,128]{1,0:T(8,128)S(1)}, u32[]{:S(2)}, u32[]{:S(2)}) %collective-permute-start) | collective-permute-done | bytes 147488 | tf_op jit(solution)/shard_map/ppermute | solution.py:448
  20.1 0.9 %collective-permute-done.1.got2 = f32[288,128]{1,0:T(8,128)S(1)} collective-permute-done((f32[288,128]{1,0:T(8,128)S(1)}, f32[288,128]{1,0:T(8,128)S(1)}, u32[]{:S(2)}, u32[]{:S(2)}) %collective-permute-start.1) | collective-permute-done | bytes 147488 | tf_op jit(solution)/shard_map/ppermute | solution.py:448
  21.0 0.5 %pack_lat.1 = (f32[23,8,128]{2,1,0:T(8,128)S(1)}, f32[23,8,128]{2,1,0:T(8,128)S(1)}) custom-call(f32[12,4,128,128]{3,2,1,0:T(8,128)S(1)} %rotate_main.1.main, f32[288,128]{1,0:T(8,128)S(1)} %collective-permute-done.got1, f32[288,128]{1,0:T(8,128)S(1)} %collective-permute-done.1.got2), custom_call_target="tpu_custom_call" | custom-call | flops 1000000 | bytes 4194304 | tf_op jit(solution)/shard_map/pack_lat/pallas_call | solution.py:432
  21.5 6.2 %collective-permute-start.2 = (f32[23,8,128]{2,1,0:T(8,128)S(1)}, f32[23,8,128]{2,1,0:T(8,128)S(1)}, u32[]{:S(2)}, u32[]{:S(2)}) collective-permute-start(f32[23,8,128]{2,1,0:T(8,128)S(1)} %get-tuple-element.22.token), channel_id=1, source_target_pairs={{1,2},{2,1},{3,4},{4,3},{5,6},{6,5},{7,8},{8,7},{9,10},{10,9},{11,... | collective-permute-start | bytes 282632 | tf_op jit(solution)/shard_map/ppermute | solution.py:460
  27.7 3.7 %inner.1 = (f32[9,2,5,8,128]{4,3,2,1,0:T(8,128)S(1)}, f32[3,2,5,8,128]{4,3,2,1,0:T(8,128)S(1)}, f32[8,2,5,8,128]{4,3,2,1,0:T(8,128)S(1)}, f32[4,128,128]{2,1,0:T(8,128)S(1)}, f32[2,4,8,128]{3,2,1,0:T(8,128)S(1)}) custom-call(f32[12,4,128,128]{3,2,1,0:T(8,128)S(1)} %rotate_main.1.main, f32[288,128]{1,0:T(8,128)S(1)} %collective-permute-done.got1, ...), custom_call_target="tpu_custom_call" | custom-call | flops 30000000 | bytes 4194304 | tf_op jit(solution)/shard_map/inner/pallas_call | solution.py:432
  31.4 1.9 %all-gather = f32[46,8,128]{2,1,0:T(8,128)S(1)} all-gather(f32[23,8,128]{2,1,0:T(8,128)S(1)} %get-tuple-element.28), channel_id=2, replica_groups={{0,1},{2,3},{4,5},{6,7},{8,9},{10,11},{12,13},{14,15},{16,17},{18,19},{..., dimensions={0}, use_global_device_ids=true | all-gather | bytes 282624 | tf_op jit(solution)/shard_map/all_gather | solution.py:452
  33.3 0.0 collective-permute-done.2.got2
  33.3 1.7 %finish.1 = f32[4,128,128]{2,1,0:T(8,128)} custom-call(f32[9,2,5,8,128]{4,3,2,1,0:T(8,128)S(1)} %get-tuple-element.23.edge_coef, f32[3,2,5,8,128]{4,3,2,1,0:T(8,128)S(1)} %get-tuple-element.24.edge_field, f32[8,2,5,8,128]{4,3,2,1,0:T(8,128)S(1)} %get-tuple-element.25.saved, f32[4,128,128]{2,1,0:T(8,128)S(1)} %get-tuple-element.26.result, ...), custom_call_target="tpu_custom_call" | custom-call | flops 1000000 | bytes 4194304 | tf_op jit(solution)/shard_map/finish/pallas_call | solution.py:432
Async XLA Ops:
  2.0 18.1 %collective-permute-start = (f32[288,128]{1,0:T(8,128)S(1)}, f32[288,128]{1,0:T(8,128)S(1)}, u32[]{:S(2)}, u32[]{:S(2)}) collective-permute-start(f32[288,128]{1,0:T(8,128)S(1)} %get-tuple-element.19.token), channel_id=1, source_target_pairs={{0,16},{16,32},{32,48},{48,64},{64,80},{80,96},{96,112},{112,128},... | collective-permute-start | bytes 442376 | tf_op jit(solution)/shard_map/ppermute | solution.py:448
  6.1 14.9 %collective-permute-start.1 = (f32[288,128]{1,0:T(8,128)S(1)}, f32[288,128]{1,0:T(8,128)S(1)}, u32[]{:S(2)}, u32[]{:S(2)}) collective-permute-start(f32[288,128]{1,0:T(8,128)S(1)} %get-tuple-element.20), channel_id=1, source_target_pairs={{0,496},{16,0},{32,16},{48,32},{64,48},{80,64},{96,80},{112,96},{1... | collective-permute-start | bytes 442376 | tf_op jit(solution)/shard_map/ppermute | solution.py:448
  21.5 11.8 %collective-permute-start.2 = (f32[23,8,128]{2,1,0:T(8,128)S(1)}, f32[23,8,128]{2,1,0:T(8,128)S(1)}, u32[]{:S(2)}, u32[]{:S(2)}) collective-permute-start(f32[23,8,128]{2,1,0:T(8,128)S(1)} %get-tuple-element.22.token), channel_id=1, source_target_pairs={{1,2},{2,1},{3,4},{4,3},{5,6},{6,5},{7,8},{8,7},{9,10},{10,9},{11,... | collective-permute-start | bytes 282632 | tf_op jit(solution)/shard_map/ppermute | solution.py:460
